TPU v7x, 128 devices: a whole 4x4x4 slice. The times are simulated.
128 devices in a mesh: dp: 32 (over x, y, z_lo), tensor: 4 (over z_hi, core).
Axes of the slice: x: 4, y: 4, z: 4 (z_hi: 2, z_lo: 2; z = z_hi * 2 + z_lo), core: 2. Of those that a mesh axis runs over, the one named last changes fastest.
Arguments:
- hidden_in: bfloat16 [32768, 1536], P(('dp', 'tensor')), may hold values from -6 to 6
- norm_gain: bfloat16 [1536], replicated, may hold values from 0.5 to 1.5
- w_z: bfloat16 [1536, 3072], P('dp', 'tensor'), may hold values from -0.15625 to 0.15625
- w_x: bfloat16 [1536, 3072], P('dp', 'tensor'), may hold values from -0.15625 to 0.15625
- w_bc: bfloat16 [1536, 256], P('dp'), may hold values from -0.15625 to 0.15625
- w_dt: bfloat16 [1536, 48], P('dp', 'tensor'), may hold values from -0.15625 to 0.15625
- conv_x: bfloat16 [4, 3072], P(None, 'tensor'), may hold values from -3 to 3
- conv_x_bias: bfloat16 [3072], P('tensor'), may hold values from -3 to 3
- conv_bc: bfloat16 [4, 256], replicated, may hold values from -3 to 3
- conv_bc_bias: bfloat16 [256], replicated, may hold values from -3 to 3
- dt_bias: float32 [48], P('tensor'), may hold values from -6 to -1.5
- a_log: float32 [48], P('tensor'), may hold values from -3 to 1
- skip_d: float32 [48], P('tensor'), may hold values from 0.5 to 1.5
- gate_norm: bfloat16 [3072], P('tensor'), may hold values from 0.5 to 1.5
- w_out: bfloat16 [3072, 1536], P('tensor', 'dp'), may hold values from -0.109375 to 0.109375
- lengths: int32 [32, 4], P('dp'), may hold values from 0 to 1024, as said below
- out_grad: bfloat16 [32768, 1536], P(('dp', 'tensor')), may hold values from -24 to 24
Outputs:
- block_out: float32 [32768, 1536], P(('dp', 'tensor'))
- input_grad: float32 [32768, 1536], P(('dp', 'tensor'))
- norm_gain_grad: float32 [1536], replicated
- w_z_grad: float32 [1536, 3072], P('dp', 'tensor')
- w_x_grad: float32 [1536, 3072], P('dp', 'tensor')
- w_bc_grad: float32 [1536, 256], P('dp')
- w_dt_grad: float32 [1536, 48], P('dp', 'tensor')
- conv_x_grad: float32 [4, 3072], P(None, 'tensor')
- conv_x_bias_grad: float32 [3072], P('tensor')
- conv_bc_grad: float32 [4, 256], replicated
- conv_bc_bias_grad: float32 [256], replicated
- dt_bias_grad: float32 [48], P('tensor')
- a_log_grad: float32 [48], P('tensor')
- skip_d_grad: float32 [48], P('tensor')
- gate_norm_grad: float32 [3072], P('tensor')
- w_out_grad: float32 [3072, 1536], P('tensor', 'dp')
Inputs may be any that keep to these rules, and one draw needn't show every extreme that they name: Each group's lengths sum to 1024 or less; one of them is 770 or more and starts within the group's first 256 rows; in every draw some group is one sequence of exactly 1024; lengths of 0 occur.
All inputs are finite; a program needn't handle non-finite values.
Results may differ from a plain program's by a relative error of at most 0.011.
Values may be sent and summed in bfloat16 or wider, within the bound.
A program may use at most 128 MiB of HBM per device.

v0:
```python
from functools import partial

import jax
import jax.numpy as jnp
from jax import lax
from jax.sharding import PartitionSpec as P

HEAD_DIM = 64
STATE = 128
KERNEL = 4
STRETCH = 256
INNER = 3072


highest = lax.Precision.HIGHEST
epsilon = 1e-05


def silu_of(values):
    return values * jax.nn.sigmoid(values)


def dot_last(left, right):
    return lax.dot_general(
        left, right, (((1,), (1,)), ((), ())), preferred_element_type=jnp.float32
    )


def dot_first(left, right):
    return lax.dot_general(
        left, right, (((0,), (0,)), ((), ())), preferred_element_type=jnp.float32
    )


def segment_ids(lengths_row, total_rows):
    seq_ends = jnp.cumsum(lengths_row)
    places = jnp.arange(total_rows, dtype=jnp.int32)
    seg_ids = jnp.sum((places[:, None] >= seq_ends[None, :]).astype(jnp.int32), axis=1)
    alive = (places < seq_ends[-1]).astype(jnp.float32)
    return (seg_ids, alive)


def causal_conv(values, kernel, kernel_bias, seg_ids):
    total_rows = values.shape[0]
    summed = kernel_bias[None, :] + kernel[KERNEL - 1][None, :] * values
    for offset in range(1, KERNEL):
        moved = jnp.concatenate(
            [jnp.zeros((offset, values.shape[1]), jnp.float32), values[: total_rows - offset]],
            axis=0,
        )
        moved_ids = jnp.concatenate(
            [jnp.full((offset,), -1, jnp.int32), seg_ids[: total_rows - offset]]
        )
        same_seq = (moved_ids == seg_ids).astype(jnp.float32)
        summed = summed + kernel[KERNEL - 1 - offset][None, :] * moved * same_seq[:, None]
    return silu_of(summed)


def state_scan(values, steps, b_proj, c_proj, seg_ids, rates):
    total_rows, heads, width = values.shape
    blocks = total_rows // STRETCH
    block_values = values.reshape(blocks, STRETCH, heads, width)
    block_steps = steps.reshape(blocks, STRETCH, heads)
    block_b = b_proj.reshape(blocks, STRETCH, STATE)
    block_c = c_proj.reshape(blocks, STRETCH, STATE)
    block_ids = seg_ids.reshape(blocks, STRETCH)
    earlier = jnp.concatenate([jnp.full((1,), -1, jnp.int32), block_ids[:-1, STRETCH - 1]])
    positions = jnp.arange(STRETCH, dtype=jnp.int32)
    causal = positions[:, None] >= positions[None, :]

    def advance(carried, pieces):
        part_values, part_steps, part_b, part_c, part_ids, before_id = pieces
        log_decay = jnp.cumsum(part_steps * rates[None, :], axis=0)
        same_seq = (part_ids[:, None] == part_ids[None, :]) & causal
        spans = log_decay[:, None, :] - log_decay[None, :, :]
        decays = jnp.exp(jnp.where(same_seq[:, :, None], spans, -jnp.inf))
        scores = lax.dot_general(
            part_c,
            part_b,
            (((1,), (1,)), ((), ())),
            precision=highest,
            preferred_element_type=jnp.float32,
        )
        mixing = scores[:, :, None] * decays * part_steps[None, :, :]
        result = jnp.einsum("tsh,shp->thp", mixing, part_values, precision=highest)
        inherit = (part_ids == before_id).astype(jnp.float32)
        readout = jnp.einsum("tn,hpn->thp", part_c, carried, precision=highest)
        result = result + jnp.exp(log_decay)[:, :, None] * inherit[:, None, None] * readout
        last_id = part_ids[STRETCH - 1]
        tail_same = (part_ids == last_id).astype(jnp.float32)
        towards = (
            jnp.exp(log_decay[STRETCH - 1][None, :] - log_decay) * tail_same[:, None] * part_steps
        )
        fresh = jnp.einsum(
            "shp,sn->hpn", towards[:, :, None] * part_values, part_b, precision=highest
        )
        keep_state = (last_id == before_id).astype(jnp.float32)
        carried = keep_state * jnp.exp(log_decay[STRETCH - 1])[:, None, None] * carried + fresh
        return (carried, result)

    initial = jnp.zeros((heads, width, STATE), jnp.float32)
    leftover, outputs = lax.scan(
        jax.checkpoint(advance),
        initial,
        (block_values, block_steps, block_b, block_c, block_ids, earlier),
    )
    return outputs.reshape(total_rows, heads, width)


def mixer(
    seg_ids,
    inner_x,
    inner_bc,
    step_raw,
    kernel_x,
    bias_x,
    kernel_bc,
    bias_bc,
    step_bias,
    log_rate,
    skip_gain,
):
    conv_out = causal_conv(inner_x, kernel_x, bias_x, seg_ids)
    bc_out = causal_conv(inner_bc, kernel_bc, bias_bc, seg_ids)
    step_sizes = jax.nn.softplus(step_raw + step_bias[None, :])
    rates = -jnp.exp(log_rate)
    total_rows = inner_x.shape[0]
    heads = step_bias.shape[0]
    values = conv_out.reshape(total_rows, heads, HEAD_DIM)
    result = (
        state_scan(values, step_sizes, bc_out[:, :STATE], bc_out[:, STATE:], seg_ids, rates)
        + skip_gain[None, :, None] * values
    )
    return result.reshape(total_rows, heads * HEAD_DIM)


def per_device(
    hidden_in,
    norm_gain,
    w_z,
    w_x,
    w_bc,
    w_dt,
    conv_x,
    conv_x_bias,
    conv_bc,
    conv_bc_bias,
    dt_bias,
    a_log,
    skip_d,
    gate_norm,
    w_out,
    lengths,
    out_grad,
):
    piece_rows = hidden_in.shape[0]
    my_first = lax.axis_index("tensor") * piece_rows
    inputs = hidden_in.astype(jnp.float32)
    gain_vec = norm_gain.astype(jnp.float32)
    inv_rms = lax.rsqrt(jnp.mean(inputs * inputs, axis=-1) + epsilon)
    normed = (inputs * inv_rms[:, None] * gain_vec[None, :]).astype(jnp.bfloat16)
    full_z, full_x, full_bc, full_dt, full_out = (
        lax.all_gather(w_z, "dp", axis=0, tiled=True),
        lax.all_gather(w_x, "dp", axis=0, tiled=True),
        lax.all_gather(w_bc, "dp", axis=0, tiled=True),
        lax.all_gather(w_dt, "dp", axis=0, tiled=True),
        lax.all_gather(w_out, "dp", axis=1, tiled=True),
    )
    gathered = lax.all_gather(normed, "tensor", axis=0, tiled=True)
    group_rows = gathered.shape[0]
    seg_ids, alive = segment_ids(lengths[0], group_rows)
    alive_mine = lax.dynamic_slice_in_dim(alive, my_first, piece_rows)
    gate_pre = jnp.dot(gathered, full_z, preferred_element_type=jnp.float32)
    inner_x = jnp.dot(gathered, full_x, preferred_element_type=jnp.float32)
    inner_bc = jnp.dot(gathered, full_bc, preferred_element_type=jnp.float32)
    step_raw = jnp.dot(gathered, full_dt, preferred_element_type=jnp.float32)
    mixed, pullback = jax.vjp(
        partial(mixer, seg_ids),
        inner_x,
        inner_bc,
        step_raw,
        conv_x.astype(jnp.float32),
        conv_x_bias.astype(jnp.float32),
        conv_bc.astype(jnp.float32),
        conv_bc_bias.astype(jnp.float32),
        dt_bias,
        a_log,
        skip_d,
    )
    gate_silu = silu_of(gate_pre)
    gated = mixed * gate_silu
    square_sum = lax.psum(jnp.sum(gated * gated, axis=-1), "tensor")
    inv_gated = lax.rsqrt(square_sum / INNER + epsilon)
    scaled = gated * inv_gated[:, None]
    gnorm_vec = gate_norm.astype(jnp.float32)
    normed_out = (scaled * gnorm_vec[None, :]).astype(jnp.bfloat16)
    branch_rows = lax.psum_scatter(
        jnp.dot(normed_out, full_out, preferred_element_type=jnp.float32).astype(jnp.bfloat16),
        "tensor",
        scatter_dimension=0,
        tiled=True,
    ).astype(jnp.float32)
    block_out = inputs + alive_mine[:, None] * branch_rows
    cotangent = out_grad.astype(jnp.float32)
    masked_cot = (cotangent * alive_mine[:, None]).astype(jnp.bfloat16)
    full_z, full_x, full_bc, full_dt, full_out = (
        lax.all_gather(w_z, "dp", axis=0, tiled=True),
        lax.all_gather(w_x, "dp", axis=0, tiled=True),
        lax.all_gather(w_bc, "dp", axis=0, tiled=True),
        lax.all_gather(w_dt, "dp", axis=0, tiled=True),
        lax.all_gather(w_out, "dp", axis=1, tiled=True),
    )
    all_cot = lax.all_gather(masked_cot, "tensor", axis=0, tiled=True)
    grad_normed_out = dot_last(all_cot, full_out)
    grad_w_out = dot_first(normed_out, all_cot)
    grad_gate_norm = jnp.sum(grad_normed_out * scaled, axis=0)
    grad_scaled = grad_normed_out * gnorm_vec[None, :]
    cross_sum = lax.psum(jnp.sum(grad_scaled * gated, axis=-1), "tensor")
    grad_gated = (
        inv_gated[:, None] * grad_scaled
        - gated * (inv_gated * inv_gated * inv_gated * cross_sum / INNER)[:, None]
    )
    grad_mixed = grad_gated * gate_silu
    sigmoid_gate = jax.nn.sigmoid(gate_pre)
    grad_gate = grad_gated * mixed * sigmoid_gate * (1.0 + gate_pre * (1.0 - sigmoid_gate))
    (
        grad_x,
        grad_bc,
        grad_step,
        grad_kernel_x,
        grad_bias_x,
        grad_kernel_bc,
        grad_bias_bc,
        grad_step_bias,
        grad_log_rate,
        grad_skip,
    ) = pullback(grad_mixed)
    grad_bc, grad_kernel_bc, grad_bias_bc = lax.psum(
        (grad_bc, grad_kernel_bc, grad_bias_bc), "tensor"
    )
    round_gate = grad_gate.astype(jnp.bfloat16)
    round_x = grad_x.astype(jnp.bfloat16)
    round_bc = grad_bc.astype(jnp.bfloat16)
    round_step = grad_step.astype(jnp.bfloat16)
    grad_w_z = dot_first(gathered, round_gate)
    grad_w_x = dot_first(gathered, round_x)
    grad_w_bc = dot_first(gathered, round_bc)
    grad_w_dt = dot_first(gathered, round_step)
    total = dot_last(round_gate, full_z) + dot_last(round_x, full_x)
    grad_normed = lax.psum_scatter(
        (total + dot_last(round_step, full_dt)).astype(jnp.bfloat16),
        "tensor",
        scatter_dimension=0,
        tiled=True,
    ).astype(jnp.float32)
    grad_normed = grad_normed + dot_last(
        lax.dynamic_slice_in_dim(round_bc, my_first, piece_rows), full_bc
    )
    grad_gain_part = jnp.sum(grad_normed * inputs * inv_rms[:, None], axis=0)
    grad_scaled_in = grad_normed * gain_vec[None, :]
    inner_mean = jnp.mean(grad_scaled_in * inputs, axis=-1)
    input_grad = (
        cotangent
        + inv_rms[:, None] * grad_scaled_in
        - inputs * (inv_rms * inv_rms * inv_rms * inner_mean)[:, None]
    )
    grad_gain = lax.psum(grad_gain_part, ("dp", "tensor"))
    owned_z, owned_x, owned_bc, owned_dt, owned_out = (
        lax.psum_scatter(grad_w_z, "dp", scatter_dimension=0, tiled=True),
        lax.psum_scatter(grad_w_x, "dp", scatter_dimension=0, tiled=True),
        lax.psum_scatter(grad_w_bc, "dp", scatter_dimension=0, tiled=True),
        lax.psum_scatter(grad_w_dt, "dp", scatter_dimension=0, tiled=True),
        lax.psum_scatter(grad_w_out, "dp", scatter_dimension=1, tiled=True),
    )
    summed_small = lax.psum(
        (
            grad_kernel_x,
            grad_bias_x,
            grad_kernel_bc,
            grad_bias_bc,
            grad_step_bias,
            grad_log_rate,
            grad_skip,
            grad_gate_norm,
        ),
        "dp",
    )
    return (
        block_out,
        input_grad,
        grad_gain,
        owned_z,
        owned_x,
        owned_bc,
        owned_dt,
        summed_small[0],
        summed_small[1],
        summed_small[2],
        summed_small[3],
        summed_small[4],
        summed_small[5],
        summed_small[6],
        summed_small[7],
        owned_out,
    )


def solution(mesh):
    in_specs = (
        P(("dp", "tensor"), None),
        P(),
        P("dp", "tensor"),
        P("dp", "tensor"),
        P("dp", None),
        P("dp", "tensor"),
        P(None, "tensor"),
        P("tensor"),
        P(),
        P(),
        P("tensor"),
        P("tensor"),
        P("tensor"),
        P("tensor"),
        P("tensor", "dp"),
        P("dp", None),
        P(("dp", "tensor"), None),
    )
    out_specs = (
        P(("dp", "tensor"), None),
        P(("dp", "tensor"), None),
        P(),
        P("dp", "tensor"),
        P("dp", "tensor"),
        P("dp", None),
        P("dp", "tensor"),
        P(None, "tensor"),
        P("tensor"),
        P(),
        P(),
        P("tensor"),
        P("tensor"),
        P("tensor"),
        P("tensor"),
        P("tensor", "dp"),
    )
    return jax.shard_map(
        per_device, mesh=mesh, in_specs=in_specs, out_specs=out_specs, check_vma=False
    )
```

profile of v0, /device:TPU:1, one launch (start us, length us, event | category | flops | bytes accessed | tf_op | source)
XLA Modules:
  0.0 1736.3 jit_solution(11452186093772068748)
XLA Ops:
  24.3 69.9 %all-gather = bf16[32,48,12]{1,2,0:T(8,128)(2,1)S(1)} all-gather(bf16[1,48,12]{1,2,0:T(8,128)(2,1)S(1)} %bitcast.411), channel_id=1, replica_groups=mesh['dp'=32,'tensor'=4] {'dp'}, dimensions={0}, use_global_device_ids=true | all-gather | bytes 38016 | tf_op jit(solution)/shard_map/all_gather | solution.py:166
  95.1 74.6 %all_gather.29 = bf16[1536,256]{1,0:T(8,128)(2,1)} all-gather(bf16[48,256]{1,0:T(8,128)(2,1)S(1)} %copy-done.42), channel_id=1, replica_groups=mesh['dp'=32,'tensor'=4] {'dp'}, dimensions={0}, use_global_device_ids=true | all-gather | bytes 811008 | tf_op jit(solution)/shard_map/all_gather | solution.py:165
  170.3 3.7 compare_select_fusion.2
  182.5 2.6 all-gather.9.cloned.1.call-done
  185.1 4.3 fusion.141
  189.5 4.4 fusion.99
  196.3 3.4 reshape.427
  204.2 150.0 %while.41 = (s32[]{:T(128)}, f32[12,64,128]{2,1,0:T(8,128)S(1)}, f32[4,256,12,64]{1,0,3,2:T(4,128)}, f32[4,12,64,128]{3,2,1,0:T(8,128)}, s32[4,256]{1,0:T(4,128)...) while((s32[]{:T(128)}, f32[12,64,128]{2,1,0:T(8,128)S(1)}, ...), condition=%wide.region_6.7_spmd.clone, body=%wide.region_3.6_spmd.clone.sunk | while | flops 1313456128 | bytes 10579746 | solution.py:102
  215.1 4.9 fusion.233
  223.7 17.9 %dynamic_update_slice.66 = f32[4,256,12,64]{1,0,3,2:T(4,128)} dynamic-update-slice(f32[4,256,12,64]{1,0,3,2:T(4,128)} %get-tuple-element.1146, f32[1,256,12,64]{1,0,3,2:T(1,128)S(1)} %copy.244, s32[]{:T(128)S(6)} %copy.266, s32[]{:T(128)} %constant.142.clone.1..sunk, s32[]{:T(128)} %constant.142.clone.1..sunk, s32[]{:T(128)} %constant.142.clone.1..sunk) | dynamic-update-slice | bytes 1572868 | tf_op jit(solution)/shard_map/jvp()/while/body/jit(dynamic_update_index_in_dim)/dynamic_update_slice | solution.py:102
  252.5 4.9 fusion.233
  261.1 17.9 %dynamic_update_slice.66 = f32[4,256,12,64]{1,0,3,2:T(4,128)} dynamic-update-slice(f32[4,256,12,64]{1,0,3,2:T(4,128)} %get-tuple-element.1146, f32[1,256,12,64]{1,0,3,2:T(1,128)S(1)} %copy.244, s32[]{:T(128)S(6)} %copy.266, s32[]{:T(128)} %constant.142.clone.1..sunk, s32[]{:T(128)} %constant.142.clone.1..sunk, s32[]{:T(128)} %constant.142.clone.1..sunk) | dynamic-update-slice | bytes 1572868 | tf_op jit(solution)/shard_map/jvp()/while/body/jit(dynamic_update_index_in_dim)/dynamic_update_slice | solution.py:102
  289.9 4.9 fusion.233
  298.5 17.9 %dynamic_update_slice.66 = f32[4,256,12,64]{1,0,3,2:T(4,128)} dynamic-update-slice(f32[4,256,12,64]{1,0,3,2:T(4,128)} %get-tuple-element.1146, f32[1,256,12,64]{1,0,3,2:T(1,128)S(1)} %copy.244, s32[]{:T(128)S(6)} %copy.266, s32[]{:T(128)} %constant.142.clone.1..sunk, s32[]{:T(128)} %constant.142.clone.1..sunk, s32[]{:T(128)} %constant.142.clone.1..sunk) | dynamic-update-slice | bytes 1572868 | tf_op jit(solution)/shard_map/jvp()/while/body/jit(dynamic_update_index_in_dim)/dynamic_update_slice | solution.py:102
  327.4 4.9 fusion.233
  335.9 17.9 %dynamic_update_slice.66 = f32[4,256,12,64]{1,0,3,2:T(4,128)} dynamic-update-slice(f32[4,256,12,64]{1,0,3,2:T(4,128)} %get-tuple-element.1146, f32[1,256,12,64]{1,0,3,2:T(1,128)S(1)} %copy.244, s32[]{:T(128)S(6)} %copy.266, s32[]{:T(128)} %constant.142.clone.1..sunk, s32[]{:T(128)} %constant.142.clone.1..sunk, s32[]{:T(128)} %constant.142.clone.1..sunk) | dynamic-update-slice | bytes 1572868 | tf_op jit(solution)/shard_map/jvp()/while/body/jit(dynamic_update_index_in_dim)/dynamic_update_slice | solution.py:102
  354.2 4.4 copy.222
  358.6 3.8 copy.161
  362.4 9.7 multiply_reduce_fusion.10
  372.1 30.5 %psum.98 = f32[1024]{0:T(1024)S(1)} all-reduce(f32[1024]{0:T(1024)S(1)} %get-tuple-element.838), channel_id=1, replica_groups=mesh['dp'=32,'tensor'=4] {'tensor'}, use_global_device_ids=true, to_apply=%region_8.9 | all-reduce | flops 1024 | bytes 8192 | tf_op jit(solution)/shard_map/psum | solution.py:192
  402.6 94.3 %all-gather.13.cloned.1.call-done = bf16[768,1536]{0,1:T(8,128)(2,1)} async-done(((bf16[768,48]{0,1:T(8,128)(2,1)}), bf16[768,1536]{0,1:T(8,128)(2,1)}) %all-gather.13.cloned.1.call-update) | async-done | bytes 2359312 | tf_op jit(solution)/shard_map/all_gather | solution.py:167
  496.9 55.1 %all-gather.15.cloned.1.call-done = bf16[1024,1536]{1,0:T(8,128)(2,1)} async-done(((bf16[256,1536]{1,0:T(8,128)(2,1)}), bf16[1024,1536]{1,0:T(8,128)(2,1)}) %all-gather.15.cloned.1.call-update) | async-done | bytes 3145744 | tf_op jit(solution)/shard_map/all_gather | solution.py:213
  552.0 8.5 multiply_reduce_fusion.3
  560.5 6.8 psum.99
  567.3 8.1 multiply_reduce_fusion.4
  577.7 3.0 reshape.431
  585.4 233.6 %while.42 = (s32[]{:T(128)}, f32[12]{0:T(128)}, f32[12,64,128]{2,1,0:T(8,128)S(1)}, f32[4,256,12,64]{1,0,3,2:T(4,128)}, f32[4,256,12]{1,0,2:T(4,128)}, /*index=5...) while((s32[]{:T(128)}, f32[12]{0:T(128)}, ...), condition=%wide.region_26.27_spmd.clone, body=%wide.region_12.26_spmd.clone.sunk | while | flops 3036590080 | bytes 26342644 | solution.py:102
  590.2 2.7 constant_dynamic-slice_fusion.7
  601.6 5.4 fusion.253
  609.4 2.8 fusion.257
  617.5 2.5 reduce-window.80
  625.5 17.8 %dynamic_update_slice.69 = f32[4,256,12,64]{1,0,3,2:T(4,128)} dynamic-update-slice(f32[4,256,12,64]{1,0,3,2:T(4,128)} %get-tuple-element.1197, f32[1,256,12,64]{1,0,3,2:T(1,128)S(1)} %copy.254, s32[]{:T(128)S(6)} %sub.289, s32[]{:T(128)} %constant.142.clone.1..sunk.1, s32[]{:T(128)} %constant.142.clone.1..sunk.1, s32[]{:T(128)} %constant.142.clone.1..sunk.1) | dynamic-update-slice | bytes 1572868 | tf_op jit(solution)/shard_map/transpose(jvp())/while/body/jit(dynamic_update_index_in_dim)/dynamic_update_slice | solution.py:102
  648.0 2.7 constant_dynamic-slice_fusion.7
  659.4 5.4 fusion.253
  667.2 2.8 fusion.257
  675.2 2.5 reduce-window.80
  683.9 17.8 %dynamic_update_slice.69 = f32[4,256,12,64]{1,0,3,2:T(4,128)} dynamic-update-slice(f32[4,256,12,64]{1,0,3,2:T(4,128)} %get-tuple-element.1197, f32[1,256,12,64]{1,0,3,2:T(1,128)S(1)} %copy.254, s32[]{:T(128)S(6)} %sub.289, s32[]{:T(128)} %constant.142.clone.1..sunk.1, s32[]{:T(128)} %constant.142.clone.1..sunk.1, s32[]{:T(128)} %constant.142.clone.1..sunk.1) | dynamic-update-slice | bytes 1572868 | tf_op jit(solution)/shard_map/transpose(jvp())/while/body/jit(dynamic_update_index_in_dim)/dynamic_update_slice | solution.py:102
  706.4 2.7 constant_dynamic-slice_fusion.7
  717.8 5.4 fusion.253
  725.6 2.8 fusion.257
  742.3 17.8 %dynamic_update_slice.69 = f32[4,256,12,64]{1,0,3,2:T(4,128)} dynamic-update-slice(f32[4,256,12,64]{1,0,3,2:T(4,128)} %get-tuple-element.1197, f32[1,256,12,64]{1,0,3,2:T(1,128)S(1)} %copy.254, s32[]{:T(128)S(6)} %sub.289, s32[]{:T(128)} %constant.142.clone.1..sunk.1, s32[]{:T(128)} %constant.142.clone.1..sunk.1, s32[]{:T(128)} %constant.142.clone.1..sunk.1) | dynamic-update-slice | bytes 1572868 | tf_op jit(solution)/shard_map/transpose(jvp())/while/body/jit(dynamic_update_index_in_dim)/dynamic_update_slice | solution.py:102
  764.9 2.7 constant_dynamic-slice_fusion.7
  776.3 5.4 fusion.253
  784.1 2.8 fusion.257
  800.8 17.8 %dynamic_update_slice.69 = f32[4,256,12,64]{1,0,3,2:T(4,128)} dynamic-update-slice(f32[4,256,12,64]{1,0,3,2:T(4,128)} %get-tuple-element.1197, f32[1,256,12,64]{1,0,3,2:T(1,128)S(1)} %copy.254, s32[]{:T(128)S(6)} %sub.289, s32[]{:T(128)} %constant.142.clone.1..sunk.1, s32[]{:T(128)} %constant.142.clone.1..sunk.1, s32[]{:T(128)} %constant.142.clone.1..sunk.1) | dynamic-update-slice | bytes 1572868 | tf_op jit(solution)/shard_map/transpose(jvp())/while/body/jit(dynamic_update_index_in_dim)/dynamic_update_slice | solution.py:102
  820.8 4.0 fusion.117
  827.3 3.7 copy.167
  831.0 5.0 multiply_reduce_fusion.8
  842.0 2.6 fusion.143
  844.7 2.6 fusion.144
  847.3 2.7 add_convert_fusion
  852.0 5.9 convolution_convert_fusion
  862.1 33.8 %all-reduce.29 = (bf16[1024,256]{1,0:T(8,128)(2,1)}, f32[4,256]{1,0:T(4,128)S(1)}, f32[256]{0:T(256)S(1)}) all-reduce(f32[1024,256]{1,0:T(8,128)S(1)} %get-tuple-element.868, f32[4,256]{1,0:T(4,128)S(1)} %pad_add_fusion.1, f32[256]{0:T(256)S(1)} %get-tuple-element.747), channel_id=1, replica_groups=mesh['dp'=32,'tensor'=4] {'tensor'}, use_global_device_ids=true, to_apply=%region_28.29 | all-reduce | flops 263424 | bytes 1583104 | tf_op jit(solution)/shard_map/psum | solution.py:238
  895.9 4.3 fusion.147
  900.3 6.9 fusion.129
  909.1 5.7 fusion.145
  914.9 5.8 fusion.146
  921.7 130.5 %all-reduce.26 = (f32[4,768]{1,0:T(4,128)}, f32[768]{0:T(1024)}, f32[4,256]{1,0:T(4,128)}, f32[256]{0:T(256)}, f32[12]{0:T(128)}, /*index=5*/f32[12]{0:T(128)}, f32[12]{0:T(128)}, f32[768]{0:T(1024)}) all-reduce(f32[4,768]{1,0:T(4,128)S(1)} %pad_add_fusion, ...), channel_id=1, replica_groups=mesh['dp'=32,'tensor'=4] {'dp'}, use_global_device_ids=true, to_apply=%region_40.41 | all-reduce | flops 5924 | bytes 47392 | tf_op jit(solution)/shard_map/psum | solution.py:275
  1055.7 87.6 %psum.101 = f32[1536]{0:T(1024)} all-reduce(f32[1536]{0:T(1024)S(1)} %get-tuple-element.745), channel_id=1, replica_groups=mesh['dp'=32,'tensor'=4] {'dp','tensor'}, use_global_device_ids=true, to_apply=%region_31.32 | all-reduce | flops 1536 | bytes 12288 | tf_op jit(solution)/shard_map/psum | solution.py:267
  1143.3 3.4 fusion.101
  1146.7 72.7 %reduce-scatter.18.cloned.1.call-done = f32[48,256]{1,0:T(8,128)} async-done(((f32[1536,256]{1,0:T(8,128)}), f32[48,256]{1,0:T(8,128)}) %reduce-scatter.18.cloned.1.call-update) | async-done | bytes 49168 | tf_op jit(solution)/shard_map/reduce_scatter | solution.py:271
  1219.5 171.2 %reduce-scatter.20.cloned.1.call-done = f32[768,48]{0,1:T(8,128)} async-done(((f32[768,1536]{0,1:T(8,128)}), f32[768,48]{0,1:T(8,128)}) %reduce-scatter.20.cloned.1.call-update) | async-done | bytes 147472 | tf_op jit(solution)/shard_map/reduce_scatter | solution.py:273
  1390.7 169.5 %reduce-scatter.14.cloned.1.call-done = f32[48,768]{1,0:T(8,128)} async-done(((f32[1536,768]{1,0:T(8,128)}), f32[48,768]{1,0:T(8,128)}) %reduce-scatter.14.cloned.1.call-update) | async-done | bytes 147472 | tf_op jit(solution)/shard_map/reduce_scatter | solution.py:269
  1560.1 169.1 %reduce-scatter.16.cloned.1.call-done = f32[48,768]{1,0:T(8,128)} async-done(((f32[1536,768]{1,0:T(8,128)}), f32[48,768]{1,0:T(8,128)}) %reduce-scatter.16.cloned.1.call-update) | async-done | bytes 147472 | tf_op jit(solution)/shard_map/reduce_scatter | solution.py:270
  (588 shorter events, 223.3 us)
Async XLA Ops:
  7.2 7.9 copy-start.75
  7.2 10.0 copy-start.15
  7.2 11.2 copy-start.76
  7.2 11.8 copy-start.77
  7.2 12.4 copy-start.69
  7.2 14.5 copy-start.70
  7.2 15.1 copy-start.65
  7.3 15.7 copy-start.72
  7.3 16.4 copy-start.66
  7.3 17.0 copy-start.67
  7.3 87.8 %copy-start.42 = (bf16[48,256]{1,0:T(8,128)(2,1)S(1)}, bf16[48,256]{1,0:T(8,128)(2,1)}, u32[]{:S(2)}) copy-start(bf16[48,256]{1,0:T(8,128)(2,1)} %param.25) | copy-start | bytes 73732
  7.3 163.0 %all-gather.7.cloned.1.call-start = ((), (), s32[]{:S(2)}) async-start(), calls=%async_computation.7 | async-start | bytes 3932160 | tf_op jit(solution)/shard_map/all_gather | solution.py:169
  13.0 172.1 %all-gather.9.cloned.1.call-start = ((), (), s32[]{:S(2)}) async-start(), calls=%async_computation.8 | async-start | bytes 2433024 | tf_op jit(solution)/shard_map/all_gather | solution.py:164
  13.7 348.6 %all-gather.11.cloned.1.call-start = ((), (), s32[]{:S(2)}) async-start(), calls=%async_computation.9 | async-start | bytes 2433024 | tf_op jit(solution)/shard_map/all_gather | solution.py:163
  14.5 482.5 %all-gather.13.cloned.1.call-start = ((), (), s32[]{:S(2)}) async-start(), calls=%async_computation.10 | async-start | bytes 2433024 | tf_op jit(solution)/shard_map/all_gather | solution.py:167
  15.0 537.0 %all-gather.15.cloned.1.call-start = ((), (), s32[]{:S(2)}) async-start(), calls=%async_computation.12 | async-start | bytes 3932160 | tf_op jit(solution)/shard_map/all_gather | solution.py:213
  18.3 1033.8 %reduce-scatter.22.cloned.1.call-start = ((), (), s32[]{:S(2)}) async-start(), calls=%async_computation.18 | async-start | bytes 811008
  24.3 165.2 %copy-start.32 = (f32[768]{0:T(1024)}, f32[768]{0:T(1024)S(1)}, u32[]{:S(2)}) copy-start(f32[768]{0:T(1024)S(1)} %get-tuple-element.749) | copy-start | bytes 9220
  170.3 19.2 %copy-start.24 = (f32[1024]{0:T(1024)}, f32[1024]{0:T(1024)S(1)}, u32[]{:S(2)}) copy-start(f32[1024]{0:T(1024)S(1)} %get-tuple-element.875) | copy-start | bytes 12292
  170.3 19.2 %copy-start.26 = (f32[1024]{0:T(1024)}, f32[1024]{0:T(1024)S(1)}, u32[]{:S(2)}) copy-start(f32[1024]{0:T(1024)S(1)} %get-tuple-element.877) | copy-start | bytes 12292
  170.3 19.2 %copy-start.28 = (f32[1024]{0:T(1024)}, f32[1024]{0:T(1024)S(1)}, u32[]{:S(2)}) copy-start(f32[1024]{0:T(1024)S(1)} %get-tuple-element.876) | copy-start | bytes 12292
  170.3 6.6 copy-start.5
  185.1 4.4 copy-start.36
  185.1 4.4 copy-start.38
  185.1 4.4 copy-start.40
  185.1 4.4 copy-start.48
  189.4 4.5 copy-start
  358.6 3.8 copy-start.4
  358.6 3.8 copy-start.34
  362.4 189.6 %copy-start.44 = (f32[768]{0:T(1024)S(1)}, f32[768]{0:T(1024)}, u32[]{:S(2)}) copy-start(f32[768]{0:T(1024)} %convert_element_type.141) | copy-start | bytes 9220
  402.6 164.7 %copy-start.46 = (f32[1024]{0:T(1024)}, f32[1024]{0:T(1024)S(1)}, u32[]{:S(2)}) copy-start(f32[1024]{0:T(1024)S(1)} %add_rsqrt_fusion) | copy-start | bytes 12292
  580.7 4.7 copy-start.8
  597.7 15.5 copy-start.22
  599.7 13.5 copy-start.9
  599.9 13.3 copy-start.23
  607.8 5.4 copy-start.11
  655.5 15.5 copy-start.22
  657.4 13.5 copy-start.9
  657.6 13.3 copy-start.23
  665.6 5.3 copy-start.11
  713.9 15.5 copy-start.22
  715.9 13.5 copy-start.9
  716.1 13.3 copy-start.23
  724.0 5.3 copy-start.11
  772.3 15.5 copy-start.22
  774.3 13.5 copy-start.9
  774.5 13.3 copy-start.23
  782.5 5.4 copy-start.11
  820.8 4.0 copy-start.7
  824.8 228.7 %reduce-scatter.12.cloned.1.call-start = ((), (), s32[]{:S(2)}) async-start(), calls=%async_computation.13 | async-start | bytes 3932160 | tf_op jit(solution)/shard_map/reduce_scatter | solution.py:250
  827.3 3.7 copy-start.35
  831.0 5.1 copy-start.41
  850.1 293.2 %reduce-scatter.10.cloned.1.call-start = ((), (), s32[]{:S(2)}) async-start(), calls=%async_computation.11 | async-start | bytes 3932160 | tf_op jit(solution)/shard_map/reduce_scatter | solution.py:197
  857.9 361.6 %reduce-scatter.18.cloned.1.call-start = ((), (), s32[]{:S(2)}) async-start(), calls=%async_computation.16 | async-start | bytes 1622016 | tf_op jit(solution)/shard_map/reduce_scatter | solution.py:271
  895.9 4.4 copy-start.14
  900.2 490.5 %reduce-scatter.20.cloned.1.call-start = ((), (), s32[]{:S(2)}) async-start(), calls=%async_computation.17 | async-start | bytes 4866048 | tf_op jit(solution)/shard_map/reduce_scatter | solution.py:273
  907.2 652.9 %reduce-scatter.14.cloned.1.call-start = ((), (), s32[]{:S(2)}) async-start(), calls=%async_computation.14 | async-start | bytes 4866048 | tf_op jit(solution)/shard_map/reduce_scatter | solution.py:269
  914.9 814.4 %reduce-scatter.16.cloned.1.call-start = ((), (), s32[]{:S(2)}) async-start(), calls=%async_computation.15 | async-start | bytes 4866048 | tf_op jit(solution)/shard_map/reduce_scatter | solution.py:270
  920.7 132.8 %copy-start.10 = (bf16[256,1536]{1,0:T(8,128)(2,1)S(1)}, bf16[256,1536]{1,0:T(8,128)(2,1)}, u32[]{:S(2)}) copy-start(bf16[256,1536]{1,0:T(8,128)(2,1)} %param.21) | copy-start | bytes 2359300
  920.7 132.8 %copy-start.31 = (f32[1536]{0:T(1024)S(1)}, f32[1536]{0:T(1024)}, u32[]{:S(2)}) copy-start(f32[1536]{0:T(1024)} %copy-done.30) | copy-start | bytes 18436
  920.7 132.8 %copy-start.54 = (f32[256]{0:T(256)S(1)}, f32[256]{0:T(256)}, u32[]{:S(2)}) copy-start(f32[256]{0:T(256)} %copy-done.53) | copy-start | bytes 3076
  920.8 222.5 %copy-start.52 = (f32[256]{0:T(256)S(1)}, f32[256]{0:T(256)}, u32[]{:S(2)}) copy-start(f32[256]{0:T(256)} %copy-done.51) | copy-start | bytes 3076
  920.8 222.5 %copy-start.16 = (bf16[256,1536]{1,0:T(8,128)(2,1)S(1)}, bf16[256,1536]{1,0:T(8,128)(2,1)}, u32[]{:S(2)}) copy-start(bf16[256,1536]{1,0:T(8,128)(2,1)} %param.37) | copy-start | bytes 2359300
  920.8 222.5 %copy-start.56 = (f32[256]{0:T(256)S(1)}, f32[256]{0:T(256)}, u32[]{:S(2)}) copy-start(f32[256]{0:T(256)} %copy-done.55) | copy-start | bytes 3076
  (39 other events, 65.9 us)
Sparse Core Ops, SparseCore 0:
  13.1 36.9 all-gather.6
  51.8 133.2 all-gather.8
  186.8 154.0 all-gather.10
  342.3 154.5 all-gather.12
  498.4 53.5 all-gather.14
  824.9 136.6 reduce-scatter.21
  964.5 67.5 reduce-scatter.11
  1034.8 44.3 reduce-scatter.9
  1082.2 137.2 reduce-scatter.17
  1222.3 168.3 reduce-scatter.19
  1393.7 166.4 reduce-scatter.13
  1563.0 166.2 reduce-scatter.15
where the time goes:
time: 1770 us; the launch traced here: 1740 us
  waiting for transfers between devices  737 us (42%)
  blocking collectives  434 us (25%)
  local copies, waits for them, and re-layouts  268 us (15%)
  matrix products  178 us (10%)
  other arithmetic  92 us (5%)
    reduce_scatter x1, waiting for transfers between devices, per_device(): lax.psum_scatter(grad_w_out, 'dp', scatter_dimension=1, tiled=True)  171 us
    reduce_scatter x1, waiting for transfers between devices, per_device(): lax.psum_scatter(grad_w_z, 'dp', scatter_dimension=0, tiled=True)  169 us
    reduce_scatter x1, waiting for transfers between devices, per_device(): lax.psum_scatter(grad_w_x, 'dp', scatter_dimension=0, tiled=True)  169 us
    dynamic_update_slice x24, local copies, waits for them, and re-layouts, state_scan(): lax.scan(jax.checkpoint(advance), initial, (block_values, block_steps, bl...  155 us
    psum x1, blocking collectives, per_device(): lax.psum((grad_kernel_x, grad_bias_x, grad_kernel_bc, grad_bias_bc, grad_...  130 us
    all_gather x1, waiting for transfers between devices, per_device(): lax.all_gather(w_out, 'dp', axis=1, tiled=True)  94.3 us
    psum x1, blocking collectives, per_device(): grad_gain = lax.psum(grad_gain_part, ('dp', 'tensor'))  87.6 us
    all_gather x1, blocking collectives, per_device(): lax.all_gather(w_bc, 'dp', axis=0, tiled=True)  74.6 us
  transfers between devices with their start and end apart: 12, of which 7 were waited for; matrix products, arithmetic and copies ran while one was open for 15% of the time, Pallas kernels for 0%

commit v1 on v0

v1 whole, which is shorter than its diff:
```python
import jax
import jax.numpy as jnp
from jax import lax
from jax.experimental import pallas as pl
from jax.experimental.pallas import tpu as pltpu
from jax.sharding import PartitionSpec as P

f32=jnp.float32; bf16=jnp.bfloat16
T=1024; L=256; NC=4; D=1536; W=768; NP=6; N=128; HALO=8
HI=lax.Precision.HIGHEST
NEG=-1e30

def nn(a,b,prec=None): return lax.dot_general(a,b,(((1,),(0,)),((),())),precision=prec,preferred_element_type=f32)
def nt(a,b,prec=None): return lax.dot_general(a,b,(((1,),(1,)),((),())),precision=prec,preferred_element_type=f32)
def tn(a,b,prec=None): return lax.dot_general(a,b,(((0,),(0,)),((),())),precision=prec,preferred_element_type=f32)

def iota(shape,d): return lax.broadcasted_iota(jnp.int32,shape,d)
def seg_of(idx,ends):
    s=(idx>=ends[0]).astype(jnp.int32)
    for k in range(1,4): s=s+(idx>=ends[k]).astype(jnp.int32)
    return s
def sig(v): return 0.5*jnp.tanh(0.5*v)+0.5
def softplus(v): return jnp.maximum(v,0.0)+jnp.log1p(jnp.exp(-jnp.abs(v)))

def chunk_masks(ends,r0):
    ri=iota((L,128),0)+r0
    sg=seg_of(ri,ends)
    return sg,[None]+[(seg_of(ri-j,ends)==sg) for j in (1,2,3)]
def pair_cols(a,j,lo):
    return jnp.where(lo,a[:,2*j:2*j+1],a[:,2*j+1:2*j+2])
def taps(w,masks,halo):
    out=[w[halo:halo+L]]
    for q in (1,2,3):
        out.append(jnp.where(masks[q],w[halo-q:halo-q+L],0.0))
    return out
def conv_pre(ws,pv,kcols):
    s=pv[4:5,kcols]+pv[3:4,kcols]*ws[0]
    for q in (1,2,3): s=s+pv[3-q:4-q,kcols]*ws[q]
    return s

def head_steps(sraw,hv):
    dtp=sraw+hv[0:1,:]
    dt=softplus(dtp)
    return dtp,dt
def chunk_decay(ends,r0,dt,hv,ltri):
    dA=dt*hv[1:2,:]
    cs=nn(ltri,dA,HI)
    return dA,cs
def seg_scalars(ends,r0):
    before=seg_of(r0-1,ends); last=seg_of(r0+L-1,ends)
    return before,last
def chunk_state_decays(cs,sg,before,last):
    e=jnp.where(sg==before,jnp.exp(cs),0.0)
    csl=cs[L-1:L,:]
    w=jnp.where(sg==last,jnp.exp(csl-cs),0.0)
    kd=jnp.exp(csl)*jnp.where(before==last,1.0,0.0)
    return e,w,kd

def fwd_chunk(c,ends,nx,wa,pv,pb,hv,ix16,ixh,tmp,ibc,sraw,pre,mixed,yi,sin,bc16,S):
    r0=pl.multiple_of(c*L,L); rp=pl.multiple_of(c*L+HALO,8)
    rows=pl.ds(r0,L); rows_p=pl.ds(rp,L)
    n=nx[c]
    t=nn(n,wa[:,:,:,0:W].reshape(D,W))
    tmp[...]=t
    ix16[pl.ds(pl.multiple_of(c*L+16,16),L),:]=t.astype(bf16)
    t=nn(n,wa[:,:,:,W:].reshape(D,384))
    ibc[rows_p,:]=t[:,:256]
    sraw[rows,:]=t[:,256:]
    lane=iota((L,128),1); lo=lane<64
    sg,masks=chunk_masks(ends,r0)
    ti=iota((L,L),0); si=iota((L,L),1)
    mask=(seg_of(ti+r0,ends)==seg_of(si+r0,ends))&(ti>=si)
    ltri=(ti>=si).astype(f32)
    dtp,dt=head_steps(sraw[rows,:],hv)
    dA,cs=chunk_decay(ends,r0,dt,hv,ltri)
    csT=cs.T
    before,last=seg_scalars(ends,r0)
    e,w,kd=chunk_state_decays(cs,sg,before,last)
    win=pl.ds(r0,L+HALO)
    bc=[]
    for k in range(2):
        cols=slice(128*k,128*k+128)
        p=conv_pre(taps(ibc[win,cols],masks,HALO),pb,cols)
        v=(p*sig(p)).astype(bf16)
        bc16[rows,cols]=v
        bc.append(v)
    B,C=bc
    BT=B.T
    sc=nt(C,B)
    for j in range(NP):
        cols=slice(128*j,128*j+128)
        p=conv_pre(taps(jnp.concatenate([ixh[:,cols],tmp[:,cols]],axis=0),masks,HALO),pv,cols)
        ixh[:,cols]=tmp[L-HALO:L,cols]
        pre[rows,cols]=p
        xc=p*sig(p)
        u=pair_cols(dt,j,lo)*xc
        ub=u.astype(bf16)
        y=None
        for q in range(2):
            h=2*j+q
            dec=jnp.exp(jnp.where(mask,cs[:,h:h+1]-csT[h:h+1,:],NEG))
            M=(sc*dec).astype(bf16)
            uq=jnp.where(lo if q==0 else ~lo,ub,jnp.zeros_like(ub))
            t=nn(M,uq)
            y=t if y is None else y+t
        yi[rows,cols]=y
        Sj=S[:,cols]
        Sb=Sj.astype(bf16)
        sin[c,:,cols]=Sb
        y=y+pair_cols(e,j,lo)*nn(C,Sb)
        mixed[rows,cols]=y+pv[6:7,cols]*xc
        uw=(u*pair_cols(w,j,lo)).astype(bf16)
        S[:,cols]=pair_cols(kd,j,lo[:1])*Sj+nn(BT,uw)

def bwd_chunk(c,ends,pv,pb,hv,ix16,ibc,sraw,pre,mixed,yi,sin,bc16,gm,dS,
              q1,q3,dpre,rx,dbc,rstep,dk,hs):
    r0=pl.multiple_of(c*L,L)
    rows=pl.ds(r0,L)
    lane=iota((L,128),1); lo=lane<64
    sg,masks=chunk_masks(ends,r0)
    ri=iota((L,128),0)+r0
    up=[None]+[((seg_of(ri+j,ends)==sg)&(ri+j<T)) for j in (1,2,3)]
    ti=iota((L,L),0); si=iota((L,L),1)
    maskT=(seg_of(ti+r0,ends)==seg_of(si+r0,ends))&(si>=ti)
    ltri=(ti>=si).astype(f32)
    dtp,dt=head_steps(sraw[rows,:],hv)
    dA,cs=chunk_decay(ends,r0,dt,hv,ltri)
    csT=cs.T
    before,last=seg_scalars(ends,r0)
    e,w,kd=chunk_state_decays(cs,sg,before,last)
    B=bc16[rows,0:128]; C=bc16[rows,128:256]
    CT=C.T
    scT=nt(B,C)
    acc=jnp.zeros((L,L),f32); dCin=jnp.zeros((L,N),f32); dBout=jnp.zeros((L,N),f32)
    win=pl.ds(r0,L+16)
    rowq=[]
    for j in range(NP):
        cols=slice(128*j,128*j+128)
        g=gm[rows,cols]; gb=g.astype(bf16)
        p=pre[rows,cols]; s=sig(p); xc=p*s
        dtx=pair_cols(dt,j,lo)
        u=dtx*xc; ub=u.astype(bf16)
        sk=pv[6:7,cols]
        du=None
        for q in range(2):
            h=2*j+q
            dec=jnp.exp(jnp.where(maskT,csT[h:h+1,:]-cs[:,h:h+1],NEG))
            M=(scT*dec).astype(bf16)
            gq=jnp.where(lo if q==0 else ~lo,gb,jnp.zeros_like(gb))
            t=nn(M,gq)
            du=t if du is None else du+t
            acc=acc+nt(ub,gq)*dec
        dSj=dS[:,cols]; dSb=dSj.astype(bf16)
        Sb=sin[c,:,cols]
        wx_=pair_cols(w,j,lo); ex=pair_cols(e,j,lo)
        duo=wx_*nn(B,dSb)
        gef=g*ex
        ge=gef.astype(bf16); uw=(u*wx_).astype(bf16)
        dCin=dCin+nt(ge,Sb)
        dBout=dBout+nt(uw,dSb)
        yij=yi[rows,cols]
        y_in=mixed[rows,cols]-yij-sk*xc
        udo=u*duo
        q1[:,cols]=(gb.astype(f32)*yij-ub.astype(f32)*du)+(g*y_in-udo)
        du=du+duo
        q3[:,cols]=xc*du
        kdj=pair_cols(kd,j,lo[:1])
        rowq.append(jnp.sum(udo,0,keepdims=True)+jnp.sum(kdj*Sb.astype(f32)*dSj,0,keepdims=True))
        dS[:,cols]=kdj*dSj+nn(CT,ge)
        dxc=dtx*du+sk*g
        dp=dxc*(s*(1.0+p*(1.0-s)))
        ws=taps(ix16[win,cols].astype(f32),masks,16)
        dk[4:5,cols]+=jnp.sum(dp,0,keepdims=True)
        dk[5:6,cols]+=jnp.sum(g*xc,0,keepdims=True)
        for t_ in range(4):
            dk[3-t_:4-t_,cols]+=jnp.sum(dp*ws[t_],0,keepdims=True)
        wd=jnp.concatenate([dp,dpre[:,cols]],axis=0)
        dpre[:,cols]=dp[0:HALO]
        dv=pv[3:4,cols]*dp
        for t_ in (1,2,3):
            dv=dv+pv[3-t_:4-t_,cols]*jnp.where(up[t_],wd[t_:t_+L],0.0)
        rx[c,:,cols]=dv.astype(bf16)
    ab=acc.astype(bf16)
    dbc[:,0:128]=nn(ab,C)+dBout
    dbc[:,128:256]=nn(ab.T,B)+dCin
    he=((iota((W,128),0)//64)==iota((W,128),1)).astype(f32)
    dcs=nn(q1[...],he,HI)
    tailv=nn(jnp.broadcast_to(jnp.concatenate(rowq,axis=1),(8,W)),he,HI)[0:1,:]
    dcs=dcs+jnp.where(iota((L,128),0)==L-1,tailv,0.0)
    ddA=nn((si>=ti).astype(f32),dcs,HI)
    ddt=nn(q3[...],he,HI)+hv[1:2,:]*ddA
    hs[1:2,:]+=jnp.sum(ddA*dA,0,keepdims=True)
    dsr=ddt*sig(dtp)
    hs[0:1,:]+=jnp.sum(dsr,0,keepdims=True)
    rstep[c]=dsr.astype(bf16)
MESH = pl.DeviceIdType.MESH


def position():
    d = lax.axis_index("dp")
    t = lax.axis_index("tensor")
    return d // 8, (d // 2) % 4, d % 2, t // 2, t % 2


def device(x, y, zl, zh, c):
    return (lax.rem(x, 4) * 8 + lax.rem(y, 4) * 2 + zl, zh * 2 + c)


class Peers:
    def __init__(self):
        self.x, self.y, self.zl, self.zh, self.c = x, y, zl, zh, c = position()
        self.along_x = [device(x + k, y, zl, zh, c) for k in (1, 2, 3)]
        self.along_y = [device(x, y + k, zl, zh, c) for k in (1, 2, 3)]
        self.pair = device(x, y, 1 - zl, zh, c)
        self.far = device(x, y, zl, 1 - zh, c)
        self.near = device(x, y, zl, zh, 1 - c)
        self.cross = device(x, y, zl, 1 - zh, 1 - c)
        self.rank = zh * 2 + c
        self.group = [self.near, self.far, self.cross]
        self.all = self.along_x + self.along_y + [self.pair, self.far, self.near, self.cross]


def greet(devices):
    barrier = pltpu.get_barrier_semaphore()
    for other in devices:
        pl.semaphore_signal(barrier, inc=1, device_id=other, device_id_type=MESH)
    pl.semaphore_wait(barrier, len(devices))


def remote(src, dst, sems, k, to):
    return pltpu.make_async_remote_copy(
        src_ref=src, dst_ref=dst, send_sem=sems.at[0, k], recv_sem=sems.at[1, k], device_id=to, device_id_type=MESH
    )


def start_all(copies):
    for copy in copies:
        copy.start()


def wait_all(copies):
    for copy in copies:
        copy.wait()


class Ring:
    def __init__(self, at, mine, line, sems, first):
        plus, minus = line[0], line[2]
        before, after = lax.rem(mine + 3, 4), lax.rem(mine + 1, 4)
        own = [at(mine, 0), at(mine, 1)]
        self.own = [
            remote(own[0], own[0], sems, first, plus),
            remote(own[1], own[1], sems, first + 1, minus),
            remote(own[1], own[1], sems, first + 2, plus),
            remote(own[0], own[0], sems, first + 3, minus),
        ]
        self.onward = [
            remote(at(before, 0), at(before, 0), sems, first + 4, plus),
            remote(at(after, 1), at(after, 1), sems, first + 5, minus),
        ]

    def start(self):
        start_all(self.own)

    def forward(self):
        for k in range(2):
            self.own[k].wait()
            self.onward[k].start()

    def finish(self):
        wait_all(self.own[2:])
        wait_all(self.onward)


class WeightGather:
    def __init__(self, pieces, full, split, sems, p):
        x, y = p.x, p.y
        cols = full.shape[3]
        a, b = pl.ds(0, split), pl.ds(split, cols - split)
        mine = pl.ds(pl.multiple_of(p.zl * 48, 16), 48)
        self.mine = mine
        self.z = remote(full.at[x, y, mine, :], full.at[x, y, mine, :], sems, 0, p.pair)
        self.own = [
            pltpu.make_async_copy(piece, full.at[x, y, mine, pl.ds(at, width)], sems.at[0, 19 + k])
            for k, (piece, at, width) in enumerate(pieces)
        ]
        self.mid = []
        for k in range(3):
            ya, xb = full.at[x, y, :, a], full.at[x, y, :, b]
            self.mid.append(remote(ya, ya, sems, 1 + k, p.along_y[k]))
            self.mid.append(remote(xb, xb, sems, 4 + k, p.along_x[k]))
        self.last = [
            Ring(lambda o, h: full.at[o, pl.ds(2 * h, 2), :, a], x, p.along_x, sems, 7),
            Ring(lambda o, h: full.at[pl.ds(2 * h, 2), o, :, b], y, p.along_y, sems, 13),
        ]

    def load(self):
        start_all(self.own)

    def first(self):
        wait_all(self.own)
        self.z.start()

    def second(self):
        self.z.wait()
        start_all(self.mid)

    def third(self):
        wait_all(self.mid)
        start_all(self.last)

    def forward(self):
        for ring in self.last:
            ring.forward()

    def finish(self):
        for ring in self.last:
            ring.finish()


class WeightScatter:
    def __init__(self, part, got1, got2, got3, split, sems, p):
        x, y = p.x, p.y
        cols = got3.shape[1]
        self.part, self.got1, self.got2, self.got3, self.p = part, got1, got2, got3, p
        self.a, self.b = a, b = pl.ds(0, split), pl.ds(split, cols - split)
        mine = pl.ds(pl.multiple_of(p.zl * 48, 16), 48)
        other = pl.ds(pl.multiple_of((1 - p.zl) * 48, 16), 48)
        self.mine = mine
        self.one = []
        self.two = []
        for k in range(3):
            xk, yk = lax.rem(x + k + 1, 4), lax.rem(y + k + 1, 4)
            self.one.append(remote(part.at[xk, :, :, a], got1.at[k, :, :, a], sems, k, p.along_x[k]))
            if b.size:
                self.one.append(remote(part.at[:, yk, :, b], got1.at[k, :, :, b], sems, 3 + k, p.along_y[k]))
            self.two.append(remote(part.at[x, yk, :, a], got2.at[k, :, a], sems, 6 + k, p.along_y[k]))
            if b.size:
                self.two.append(remote(part.at[xk, y, :, b], got2.at[k, :, b], sems, 9 + k, p.along_x[k]))
        self.three = remote(part.at[x, y, other, :], got3, sems, 12, p.pair)

    def first(self):
        start_all(self.one)

    def second(self):
        wait_all(self.one)
        x, y, part, got = self.p.x, self.p.y, self.part, self.got1

        @pl.loop(0, 4)
        def _(i):
            for cut, at in ((self.a, (x, i)), (self.b, (i, y))):
                if cut.size:
                    total = part[at[0], at[1], :, cut].astype(f32)
                    for k in range(3):
                        total = total + got[k, i, :, cut].astype(f32)
                    part[at[0], at[1], :, cut] = total.astype(bf16)

        start_all(self.two)

    def third(self):
        wait_all(self.two)
        total = self.part[self.p.x, self.p.y].astype(f32)
        for k in range(3):
            total = total + self.got2[k].astype(f32)
        self.part[self.p.x, self.p.y] = total.astype(bf16)
        self.three.start()

    def finish(self):
        self.three.wait()
        return self.part[self.p.x, self.p.y, self.mine, :].astype(f32) + self.got3[...].astype(f32)


class RowGather:
    def __init__(self, own, full, sems, p):
        me, across = p.rank, (1 - p.zh) * 2 + p.c
        self.to_far = remote(own, full.at[me], sems, 0, p.far)
        self.to_near = remote(own, full.at[me], sems, 1, p.near)
        self.onward = remote(full.at[across], full.at[across], sems, 2, p.near)
        self.own = pltpu.make_async_copy(own, full.at[me], sems.at[0, 3])

    def first(self):
        self.to_far.start()
        self.to_near.start()
        self.own.start()

    def forward(self):
        self.to_far.wait()
        self.onward.start()

    def finish(self):
        self.onward.wait()


class RowScatter:
    def __init__(self, part, near, far, sems, p):
        self.part, self.near, self.far, self.p = part, near, far, p
        self.copies = [
            remote(part.at[z * 2 + 1 - p.c], near.at[k], sems, k, p.near)
            for k, z in ((0, 1 - p.zh), (1, p.zh))
        ]
        across = (1 - p.zh) * 2 + p.c
        self.across = across
        self.out = remote(part.at[across], far, sems, 2, p.far)

    def send_near(self, k):
        self.copies[k].start()

    def send_far(self):
        self.copies[0].wait()

        @pl.loop(0, 4)
        def _(k):
            rows = pl.ds(pl.multiple_of(k * 64, 64), 64)
            total = self.part[self.across, rows, :].astype(f32) + self.near[0, rows, :].astype(f32)
            self.part[self.across, rows, :] = total.astype(bf16)

        self.out.start()

    def finish(self):
        self.copies[1].wait()
        self.out.wait()

    def total(self, rows, cols):
        return (
            self.part[self.p.rank, rows, cols].astype(f32)
            + self.near[1, rows, cols].astype(f32)
            + self.far[rows, cols].astype(f32)
        )


class Exchange:
    def __init__(self, ref, me, others, sems, first, rows=None):
        at = ref.at[me] if rows is None else ref.at[me, rows]
        self.copies = [remote(at, at, sems, first + k, to) for k, to in enumerate(others)]

    def start(self):
        start_all(self.copies)

    def wait(self):
        wait_all(self.copies)


def spread(row):
    return jnp.broadcast_to(row, (128, L)).T


def row_of(total):
    return jnp.sum(total.T, axis=0, keepdims=True)


def mega_kernel(lengths, xloc, cotloc, w_z, w_x, w_bc, w_dt, w_out, norm_gain, conv_x, conv_x_bias, conv_bc, conv_bc_bias,
                dt_bias, a_log, skip_d, gate_norm,
                branch_out, gn_out, wz_grad, wx_grad, wo_grad, wbc_grad, wdt_grad, small_out,
                gain, pv, pb, hv, xg, nx, cot, wa, wz, wo, ix16, ixh, q1, q3, ibc, sraw, pre, mixed, yi, gate, gno, rgate, no, sin, bc16, rstep, S,
                dpre, dk, hs, dbc, ssx, crx, near, far, stz, got1, got2, got3,
                stb, bot3, dsend, drecv, rbc, bhalo, small, sx, sy, sz, stt, wbx,
                asem, bsem, tsem, xsem, csem, osem, gsem, esem, dsem, zsem, wsem, vsem, usem, msem, hsem):
    p = Peers()
    zh, c, me = p.zh, p.c, p.rank
    ga = WeightGather([(w_x, 0, W), (w_bc, W, 256)], wa, 640, asem, p)
    gz = WeightGather([(w_z, 0, W)], wz, 384, bsem, p)
    go = WeightGather([(w_out, 0, W)], wo, 384, tsem, p)
    ga.load()
    gz.load()
    go.load()
    dbc[0:128, 0:128] = jnp.zeros((128, 128), f32)
    dbc[0:12, 0:48] = w_dt[...].astype(f32)
    wa[p.x, p.y, ga.mine, W + 256:] = dbc[0:128, 0:128].T[0:48].astype(bf16)
    greet(p.all)
    gx = RowGather(xloc, xg, xsem, p)
    gc = RowGather(cotloc, cot, csem, p)
    ga.first()
    gx.first()
    gz.first()
    go.first()
    ends = [lengths[0, 0]]
    for k in range(1, 4):
        ends.append(ends[k - 1] + lengths[0, k])
    gain[0:1, :] = norm_gain[...].astype(f32).reshape(1, D)
    pv[0:4, :] = conv_x[...].astype(f32)
    pv[4:5, :] = conv_x_bias[...].astype(f32).reshape(1, W)
    pv[5:6, :] = gate_norm[...].astype(f32).reshape(1, W)
    skip = skip_d[...].reshape(1, 12)
    for j in range(NP):
        pv[6:7, 128 * j:128 * j + 128] = pair_cols(skip, j, iota((1, 128), 1) < 64)
    pb[0:4, :] = conv_bc[...].astype(f32)
    pb[4:5, :] = conv_bc_bias[...].astype(f32).reshape(1, 256)
    hv[...] = jnp.zeros((8, 128), f32)
    hv[0:1, 0:12] = dt_bias[...].reshape(1, 12)
    hv[1:2, 0:12] = -jnp.exp(a_log[...].reshape(1, 12))
    ixh[...] = jnp.zeros((HALO, W), f32)
    ix16[0:16, :] = jnp.zeros((16, W), bf16)
    ibc[0:HALO, :] = jnp.zeros((HALO, 256), f32)
    S[...] = jnp.zeros((N, W), f32)
    dk[...] = jnp.zeros((16, W), f32)
    hs[...] = jnp.zeros((8, 128), f32)
    small[...] = jnp.zeros((16, W), f32)
    ga.second()

    def norm_block(t):
        @pl.loop(0, 4)
        def _(k):
            rows = pl.ds(pl.multiple_of(k * 64, 64), 64)
            v = xg[t, rows, :].astype(f32)
            inv = lax.rsqrt(jnp.mean(v * v, axis=-1, keepdims=True) + 1e-05)
            nx[t, rows, :] = (v * inv * gain[0:1, :]).astype(bf16)

    gx.own.wait()
    norm_block(me)
    gx.to_near.wait()
    norm_block(zh * 2 + 1 - c)
    ga.third()
    gx.forward()
    gc.first()
    norm_block((1 - zh) * 2 + c)
    gx.finish()
    norm_block((1 - zh) * 2 + 1 - c)
    ga.forward()
    gz.second()
    ga.finish()
    gc.own.wait()
    gc.to_near.wait()
    gz.third()

    @pl.loop(0, NC)
    def _(i):
        fwd_chunk(i, ends, nx, wa, pv, pb, hv, ix16, ixh, q1, ibc, sraw, pre, mixed, yi, sin, bc16, S)

        @pl.when(i == 0)
        def _():
            gz.forward()
            go.second()

        @pl.when(i == 1)
        def _():
            gc.forward()
            go.third()

        @pl.when(i == 2)
        def _():
            go.forward()

    gz.finish()
    gc.finish()

    e_square = Exchange(ssx, me, p.group, esem, 0)
    e_cross = Exchange(crx, me, p.group, esem, 3)

    @pl.loop(0, NC)
    def _(i):
        rows = pl.ds(pl.multiple_of(i * L, L), L)
        gate[rows, :] = nn(nx[i], wz[...].reshape(D, W))
        total = jnp.zeros((L, 128), f32)
        for j in range(NP):
            cols = slice(128 * j, 128 * j + 128)
            g = gate[rows, cols]
            gated = mixed[rows, cols] * (g * sig(g))
            total = total + gated * gated
        ssx[me, :, rows] = jnp.broadcast_to(row_of(total), (8, L))

    e_square.start()
    go.finish()

    @pl.loop(0, NC)
    def _(i):
        rows = pl.ds(pl.multiple_of(i * L, L), L)
        live = iota((L, 128), 0) + i * L < ends[3]
        for j in range(2 * NP):
            cols = slice(128 * j, 128 * j + 128)
            cot[i, :, cols] = jnp.where(live, cot[i, :, cols].astype(f32), 0.0).astype(bf16)
        gno[rows, :] = nn(cot[i], wo[...].reshape(D, W))

    e_square.wait()

    def inv_of(rows):
        square = ssx[0, 0:1, rows] + ssx[1, 0:1, rows] + ssx[2, 0:1, rows] + ssx[3, 0:1, rows]
        return lax.rsqrt(square / 3072.0 + 1e-05)

    out = RowScatter(xg, near, far, osem, p)

    @pl.loop(0, NC)
    def _(i):
        t = jnp.where(i < 2, 1 - zh, zh) * 2 + jnp.where(lax.rem(i, 2) == 0, 1 - c, c)
        rows = pl.ds(pl.multiple_of(t * L, L), L)
        inv = spread(inv_of(rows))
        cross = jnp.zeros((L, 128), f32)
        for j in range(NP):
            cols = slice(128 * j, 128 * j + 128)
            g = gate[rows, cols]
            gated = mixed[rows, cols] * (g * sig(g))
            scaled = gated * inv
            gn = pv[5:6, cols]
            go = gno[rows, cols]
            no[t, :, cols] = (scaled * gn).astype(bf16)
            dk[6:7, cols] += jnp.sum(go * scaled, 0, keepdims=True)
            cross = cross + go * gn * gated
        crx[me, :, rows] = jnp.broadcast_to(row_of(cross), (8, L))
        for k in range(4):
            xg[t, :, 384 * k:384 * k + 384] = nt(no[t], wo[k].reshape(384, W)).astype(bf16)

        @pl.when(i == 0)
        def _():
            out.send_near(0)

        @pl.when(i == 2)
        def _():
            out.send_near(1)

    e_cross.start()

    def weight_part(rows_ref, grads, store):
        @pl.loop(0, 4)
        def _(b):
            left = rows_ref[:, :, pl.ds(pl.multiple_of(b * 384, 128), 384)].reshape(T, 384)
            g = grads[...].reshape(T, grads.shape[2])
            store(b, tn(left, g).astype(bf16).reshape(4, 96, grads.shape[2]))

    def store_wo(b, v):
        wo[b] = v

    weight_part(cot, no, store_wo)
    so = WeightScatter(wo, got1.at[0], got2.at[0], got3.at[0], 384, wsem, p)
    so.first()
    out.send_far()
    e_cross.wait()

    @pl.loop(0, NC)
    def _(i):
        rows = pl.ds(pl.multiple_of(i * L, L), L)
        inv_row = inv_of(rows)
        cross_row = crx[0, 0:1, rows] + crx[1, 0:1, rows] + crx[2, 0:1, rows] + crx[3, 0:1, rows]
        inv = spread(inv_row)
        back = spread(inv_row * inv_row * inv_row * cross_row / 3072.0)
        for j in range(NP):
            cols = slice(128 * j, 128 * j + 128)
            g = gate[rows, cols]
            s = sig(g)
            gs = g * s
            m = mixed[rows, cols]
            gg = inv * (gno[rows, cols] * pv[5:6, cols]) - m * gs * back
            gno[rows, cols] = gg * gs
            rgate[i, :, cols] = (gg * m * s * (1.0 + g * (1.0 - s))).astype(bf16)

    def store_z(b, v):
        stz[b] = v

    weight_part(nx, rgate, store_z)
    sz_ = WeightScatter(stz, got1.at[1], got2.at[1], got3.at[1], 384, zsem, p)
    sz_.first()

    S[...] = jnp.zeros((N, W), f32)
    dpre[...] = jnp.zeros((HALO, W), f32)
    dsend[...] = jnp.zeros((4, 512, 128), bf16)

    branch_copies = [
        pltpu.make_async_copy(gate.at[pl.ds(L * h, L), :], branch_out.at[:, pl.ds(W * h, W)], hsem.at[h]) for h in range(2)
    ]

    @pl.loop(0, NC)
    def _(i):
        bwd_chunk(NC - 1 - i, ends, pv, pb, hv, ix16, ibc, sraw, pre, mixed, yi, sin, bc16, gno,
                  S, q1, q3, dpre, no, dbc, rstep, dk, hs)
        upper = (NC - 1 - i) // 2
        part = pl.ds(pl.multiple_of(lax.rem(NC - 1 - i, 2) * L, L), L)
        half = iota((L, 128), 1) // 64
        for z in range(2):
            v = dbc[:, 128 * z:128 * z + 128]
            turned = pltpu.roll(v, 64, 1)
            for k in range(2):
                new = jnp.where(upper == k, v, turned)
                old = dsend[2 * z + k, part, :].astype(f32)
                dsend[2 * z + k, part, :] = jnp.where(half == upper, new, old).astype(bf16)

        @pl.when(i == 0)
        def _():
            so.second()
            out.finish()
            live = iota((L, 128), 0) + me * L < ends[3]
            for j in range(2 * NP):
                cols = slice(128 * j, 128 * j + 128)
                gate[L * (j // NP):L * (j // NP) + L, 128 * (j % NP):128 * (j % NP) + 128] = jnp.where(
                    live, out.total(slice(None), cols), 0.0)
            start_all(branch_copies)

        @pl.when(i == 1)
        def _():
            so.third()
            sz_.second()

        @pl.when(i == 2)
        def _():
            sz_.third()

    ranks = [zh * 2 + 1 - c, (1 - zh) * 2 + c, (1 - zh) * 2 + 1 - c]
    dcopies = [remote(dsend.at[r], drecv.at[k], dsem, k, to) for k, (r, to) in enumerate(zip(ranks, p.group))]
    start_all(dcopies)

    wo_grad[...] = so.finish()
    wz_grad[...] = sz_.finish()
    weight_part(nx, no, store_z)
    sx_ = WeightScatter(stz, got1.at[1], got2.at[1], got3.at[2], 384, vsem, p)
    sx_.first()
    wait_all(dcopies)

    bhalo[...] = jnp.zeros((HALO, 128), f32)
    tile = pl.ds(pl.multiple_of(zh * 128, 128), 128)
    half = (iota((L, 128), 1) // 64) == c

    @pl.loop(0, NC)
    def _(k):
        i = NC - 1 - k
        r0 = pl.multiple_of(i * L, L)
        part = pl.ds(pl.multiple_of(lax.rem(i, 2) * L, L), L)
        sg, masks = chunk_masks(ends, r0)
        ri = iota((L, 128), 0) + r0
        packed = dsend[me, part, :].astype(f32)
        for q in range(3):
            packed = packed + drecv[q, part, :].astype(f32)
        moved = jnp.where(i // 2 == c, packed, pltpu.roll(packed, 64, 1))
        grad = jnp.where(half, moved, 0.0)
        kernel = pb[:, tile]
        ws = taps(ibc[pl.ds(r0, L + HALO), tile], masks, HALO)
        pre_bc = kernel[4:5] + kernel[3:4] * ws[0] + kernel[2:3] * ws[1] + kernel[1:2] * ws[2] + kernel[0:1] * ws[3]
        s = sig(pre_bc)
        dp = grad * (s * (1.0 + pre_bc * (1.0 - s)))
        for t in range(4):
            cols = pl.ds(pl.multiple_of((3 - t) % 3 * 256 + zh * 128, 128), 128)
            row = 10 if t else 11
            small[row:row + 1, cols] += jnp.sum(dp * ws[t], 0, keepdims=True)
        cols = pl.ds(pl.multiple_of(256 + zh * 128, 128), 128)
        small[11:12, cols] += jnp.sum(dp, 0, keepdims=True)
        wd = jnp.concatenate([dp, bhalo[...]], axis=0)
        bhalo[...] = dp[0:HALO]
        dv = kernel[3:4] * dp
        for t in (1, 2, 3):
            same = (seg_of(ri + t, ends) == sg) & (ri + t < T)
            dv = dv + kernel[3 - t:4 - t] * jnp.where(same, wd[t:t + L], 0.0)
        rbc[0, i] = dv.astype(bf16)
        step = rstep[i].astype(f32)
        rbc[1, i] = (dv + jnp.where(half, 0.0, jnp.where(c == 0, pltpu.roll(step, 64, 1), step))).astype(bf16)

    def store_b(b, v):
        stb[b] = v

    weight_part(nx, rbc.at[1], store_b)
    low_cols = pl.ds(0, 128)
    sb_ = WeightScatter(stb, got1.at[0, :, :, :, low_cols], got2.at[0, :, :, low_cols], bot3, 128, usem, p)
    sb_.first()

    gn_sum = RowScatter(cot, near, far, gsem, p)
    small[8:10, :] = jnp.zeros((2, W), f32)

    @pl.loop(0, NC)
    def _(i):
        t = jnp.where(i < 2, 1 - zh, zh) * 2 + jnp.where(lax.rem(i, 2) == 0, 1 - c, c)
        for k in range(4):
            cols = slice(384 * k, 384 * k + 384)
            total = nt(rgate[t], wz[k].reshape(384, W))
            total = total + nt(no[t], wa[k, :, :, 0:W].reshape(384, W))
            total = total + nt(rstep[t], wa[k, :, :, W + 256:].reshape(384, 128))
            total = total + nt(rbc[0, t], wa[k, :, :, pl.ds(pl.multiple_of(W + zh * 128, 128), 128)].reshape(384, 128))
            cot[t, :, cols] = total.astype(bf16)
            weighted = jnp.sum(total * nx[t, :, cols].astype(f32), 0, keepdims=True) / gain[0:1, cols]
            small[8 + k // 2:9 + k // 2, 384 * (k % 2):384 * (k % 2) + 384] += weighted

        @pl.when(i == 0)
        def _():
            gn_sum.send_near(0)

        @pl.when(i == 1)
        def _():
            gn_sum.send_far()

        @pl.when(i == 2)
        def _():
            gn_sum.send_near(1)

    small[0:7, :] = dk[0:7, :]
    small[7:8, 0:128] = hs[0:1, :]
    small[7:8, 128:256] = hs[1:2, :]
    sx[p.x] = small[...]
    e_x = Exchange(sx, p.x, p.along_x, msem, 0)
    e_x.start()
    sx_.second()
    sb_.second()
    e_x.wait()
    sy[p.y] = sx[0] + sx[1] + sx[2] + sx[3]
    e_y = Exchange(sy, p.y, p.along_y, msem, 3)
    e_y.start()
    e_y.wait()
    sz[p.zl] = sy[0] + sy[1] + sy[2] + sy[3]
    e_z = Exchange(sz, p.zl, [p.pair], msem, 6)
    e_z.start()
    sb_.third()
    sx_.third()
    e_z.wait()
    small_out[...] = sz[0] + sz[1]
    stt[me] = small_out[8:16, :]
    e_t = Exchange(stt, me, p.group, msem, 7)
    e_t.start()
    wbx[me] = sb_.finish()
    e_b = Exchange(wbx, me, p.group, msem, 10)
    e_b.start()
    wx_grad[...] = sx_.finish()
    e_t.wait()
    small_out[8:16, :] = stt[0] + stt[1] + stt[2] + stt[3]
    e_b.wait()
    low = iota((48, 128), 1) < 64
    wbc_grad[:, 0:128] = jnp.where(low, wbx[0], wbx[1])
    wbc_grad[:, 128:256] = jnp.where(low, wbx[2], wbx[3])
    mine = wbx[me]
    wdt_grad[...] = jnp.where(c == 0, pltpu.roll(mine, 64, 1), mine)
    gn_sum.finish()
    for j in range(2 * NP):
        cols = slice(128 * j, 128 * j + 128)
        gate[L * (2 + j // NP):L * (3 + j // NP), 128 * (j % NP):128 * (j % NP) + 128] = gn_sum.total(slice(None), cols)
    gn_copies = [
        pltpu.make_async_copy(gate.at[pl.ds(L * (2 + h), L), :], gn_out.at[:, pl.ds(W * h, W)], hsem.at[2 + h])
        for h in range(2)
    ]
    start_all(gn_copies)
    wait_all(branch_copies)
    wait_all(gn_copies)


def finish_kernel(branch, gn, x_ref, cot, norm_gain, wz, wx, wo, wbc, wdt, small,
                  block_out, input_grad, gain_grad, wz_grad, wx_grad, wbc_grad, wdt_grad, conv_x, conv_x_bias, conv_bc,
                  conv_bc_bias, dt_bias, a_log, skip, gate_norm, wo_grad):
    x = x_ref[...].astype(f32)
    block_out[...] = x + branch[...]
    inv = lax.rsqrt(jnp.mean(x * x, axis=-1, keepdims=True) + 1e-05)
    g = gn[...] * norm_gain[...].astype(f32).reshape(1, D)
    inner = jnp.mean(g * x, axis=-1, keepdims=True)
    input_grad[...] = cot[...].astype(f32) + inv * g - x * (inv * inv * inv * inner)

    @pl.when(pl.program_id(0) == 0)
    def _():
        wz_grad[...] = wz[...]
        wx_grad[...] = wx[...]
        wo_grad[...] = wo[...]
        wbc_grad[...] = wbc[...]
        wdt_grad[...] = jnp.concatenate([wdt[...], jnp.zeros((80, 128), f32)], axis=0).T[0:12, 0:48]
        conv_x[...] = small[0:4, :]
        conv_x_bias[...] = small[4:5, :].reshape(W)
        he = ((iota((W, 128), 0) // 64) == iota((W, 128), 1)).astype(f32)
        sums = nn(jnp.broadcast_to(small[5:6, :], (8, W)), he, HI)
        skip[...] = sums[0:1, 0:12].reshape(12)
        gate_norm[...] = small[6:7, :].reshape(W)
        dt_bias[...] = small[7:8, 0:12].reshape(12)
        a_log[...] = small[7:8, 128:140].reshape(12)
        gain_grad[0:W] = small[8:9, :].reshape(W)
        gain_grad[W:D] = small[9:10, :].reshape(W)
        for k in range(3):
            conv_bc[k:k + 1, :] = small[10:11, 256 * k:256 * k + 256]
        conv_bc[3:4, :] = small[11:12, 0:256]
        conv_bc_bias[...] = small[11:12, 256:512].reshape(256)


vm = pl.BlockSpec(memory_space=pltpu.VMEM)
sm = pl.BlockSpec(memory_space=pltpu.SMEM)
hbm = pl.BlockSpec(memory_space=pl.ANY)
shape = jax.ShapeDtypeStruct
V = pltpu.VMEM


def sems(n):
    return pltpu.SemaphoreType.DMA((2, n))


def block(*args):
    rows4 = V((4, 256, D), bf16)
    scratch = dict(
        gain=V((8, D), f32), pv=V((16, W), f32), pb=V((8, 256), f32), hv=V((8, 128), f32), xg=rows4, nx=rows4, cot=rows4, wa=V((4, 4, 96, 1152), bf16), wz=V((4, 4, 96, W), bf16), wo=V((4, 4, 96, W), bf16),
        ix16=V((T + 16, W), bf16), ixh=V((HALO, W), f32), q1=V((L, W), f32), q3=V((L, W), f32),
        ibc=V((T + HALO, 256), f32), sraw=V((T, 128), f32), pre=V((T, W), f32), mixed=V((T, W), f32), yi=V((T, W), f32),
        gate=V((T, W), f32), gno=V((T, W), f32), rgate=V((4, L, W), bf16), no=V((4, L, W), bf16),
        sin=V((NC, N, W), bf16), bc16=V((T, 256), bf16), rstep=V((4, L, 128), bf16), S=V((N, W), f32),
        dpre=V((HALO, W), f32), dk=V((16, W), f32), hs=V((8, 128), f32), dbc=V((L, 256), f32),
        ssx=V((4, 8, T), f32), crx=V((4, 8, T), f32),
        near=V((2, L, D), bf16), far=V((L, D), bf16),
        stz=V((4, 4, 96, W), bf16), got1=V((2, 3, 4, 96, W), bf16), got2=V((2, 3, 96, W), bf16), got3=V((3, 48, W), bf16),
        stb=V((4, 4, 96, 128), bf16), bot3=V((48, 128), bf16),
        dsend=V((4, 512, 128), bf16), drecv=V((3, 512, 128), bf16), rbc=V((2, 4, L, 128), bf16), bhalo=V((HALO, 128), f32),
        small=V((16, W), f32), sx=V((4, 16, W), f32), sy=V((4, 16, W), f32), sz=V((2, 16, W), f32), stt=V((4, 8, W), f32),
        wbx=V((4, 48, 128), f32),
        asem=sems(21), bsem=sems(21), tsem=sems(21), xsem=sems(4), csem=sems(4), osem=sems(3), gsem=sems(3), esem=sems(6), dsem=sems(3),
        zsem=sems(13), wsem=sems(13), vsem=sems(13), usem=sems(13), msem=sems(13),
        hsem=pltpu.SemaphoreType.DMA((4,)),
    )
    return pl.pallas_call(
        mega_kernel,
        out_shape=[
            shape((256, D), f32), shape((256, D), f32), shape((48, W), f32), shape((48, W), f32), shape((48, W), f32),
            shape((48, 256), f32), shape((48, 128), f32), shape((16, W), f32),
        ],
        in_specs=[sm] + [hbm] * 5 + [vm, hbm] + [vm] * 9,
        out_specs=[hbm] * 2 + [vm] * 6,
        scratch_shapes=list(scratch.values()),
        compiler_params=pltpu.CompilerParams(collective_id=0, has_side_effects=True, vmem_limit_bytes=63 * 2**20),
        name="residual_block",
    )(*args)


def finish(*args):
    rows = pl.BlockSpec((64, D), lambda i: (i, 0))

    def whole(*dims):
        return pl.BlockSpec(dims, lambda i: (0,) * len(dims))

    outs = [(D,), (48, W), (48, W), (48, 256), (12, 48), (4, W), (W,), (4, 256), (256,), (12,), (12,), (12,), (W,), (48, W)]
    return pl.pallas_call(
        finish_kernel,
        grid=(4,),
        out_shape=[shape((256, D), f32)] * 2 + [shape(s, f32) for s in outs],
        in_specs=[rows] * 4 + [whole(D)] + [whole(48, W)] * 3 + [whole(48, 256), whole(48, 128), whole(16, W)],
        out_specs=[rows] * 2 + [whole(*s) for s in outs],
        name="finish",
    )(*args)


def per_device(hidden_in, norm_gain, w_z, w_x, w_bc, w_dt, conv_x, conv_x_bias, conv_bc, conv_bc_bias,
               dt_bias, a_log, skip_d, gate_norm, w_out, lengths, out_grad):
    branch, gn, wz, wx, wo, wbc, wdt, small = block(
        lengths, hidden_in, out_grad, w_z, w_x, w_bc, w_dt.T, w_out.T, norm_gain, conv_x, conv_x_bias, conv_bc, conv_bc_bias,
        dt_bias, a_log, skip_d, gate_norm)
    outs = list(finish(branch, gn, hidden_in, out_grad, norm_gain, wz, wx, wo, wbc, wdt, small))
    outs[6] = outs[6].T
    outs[15] = outs[15].T
    return tuple(outs)


def solution(mesh):
    rows, both = P(("dp", "tensor"), None), P("dp", "tensor")
    t = P("tensor")
    in_specs = (rows, P(), both, both, P("dp", None), both, P(None, "tensor"), t, P(), P(), t, t, t, t,
                P("tensor", "dp"), P("dp", None), rows)
    out_specs = (rows, rows, P(), both, both, P("dp", None), both, P(None, "tensor"), t, P(), P(), t, t, t, t,
                 P("tensor", "dp"))
    return jax.shard_map(per_device, mesh=mesh, in_specs=in_specs, out_specs=out_specs, check_vma=False)
```

time: 1770 us -> 191 us (0.11); the launches traced: 1740 us -> 191 us
  waiting for transfers between devices: 737 us -> 0 us
  blocking collectives: 434 us -> 0 us
  local copies, waits for them, and re-layouts: 268 us -> 0 us
  Pallas kernels: 0 us -> 190 us
  matrix products: 178 us -> 0 us
  other arithmetic: 92 us -> 0 us
    reduce_scatter x6 -> x0, waiting for transfers between devices: 583 us -> none  [the longest x1 171 us: per_device(): lax.psum_scatter(grad_w_out, 'dp', scatter_dimension=1, tiled=True)]
    psum x5 -> x0, blocking collectives: 289 us -> none  [the longest x1 130 us: per_device(): lax.psum((grad_kernel_x, grad_bias_x, grad_kernel_bc, grad_bias_bc, grad_...]
    pallas_call x0 -> x2, Pallas kernels: none -> 190 us  [the longest x1 184 us: block(): pl.pallas_call(mega_kernel, out_shape=[shape((256, D), f32), shape((256,...]
    dot_general x70 -> x0, matrix products: 174 us -> none  [the longest x12 52.4 us: advance(): result = jnp.einsum('tsh,shp->thp', mixing, part_values, precision=highest)]
    dynamic_update_slice x24 -> x0, local copies, waits for them, and re-layouts: 155 us -> none  [state_scan(): lax.scan(jax.checkpoint(advance), initial, (block_values, block_steps, bl...]
    all_gather x5 -> x0, waiting for transfers between devices: 152 us -> none  [the longest x1 94.3 us: per_device(): lax.all_gather(w_out, 'dp', axis=1, tiled=True)]
    all_gather x2 -> x0, blocking collectives: 145 us -> none  [the longest x1 74.6 us: per_device(): lax.all_gather(w_bc, 'dp', axis=0, tiled=True)]
    dynamic_slice x21 -> x0, local copies, waits for them, and re-layouts: 26.1 us -> none  [the longest x20 26 us: state_scan(): lax.scan(jax.checkpoint(advance), initial, (block_values, block_steps, bl...]
  transfers between devices with their start and end apart: 12 -> 0, of which waited for: 7 -> 0; matrix products, arithmetic and copies ran while one was open for 15% -> 0% of each run, Pallas kernels for 0% -> 0%
where the time goes in v1:
time: 191 us
  Pallas kernels  190 us (99%)
    pallas_call x1, Pallas kernels, block(): pl.pallas_call(mega_kernel, out_shape=[shape((256, D), f32), shape((256,...  184 us
    pallas_call x1, Pallas kernels, finish(): pl.pallas_call(finish_kernel, grid=(4,), out_shape=[shape((256, D), f32)]...  5.64 us

profile of v1, /device:TPU:1, one launch (start us, length us, event | category | flops | bytes accessed | tf_op | source)
XLA Modules:
  0.0 190.7 jit_solution(6490152038745554259)
XLA Ops:
  0.7 184.2 %residual_block.1 = (f32[256,1536]{1,0:T(8,128)}, f32[256,1536]{1,0:T(8,128)}, f32[48,768]{1,0:T(8,128)}, f32[48,768]{1,0:T(8,128)}, f32[48,768]{1,0:T(8,128)}, ...) custom-call(s32[1,4]{1,0:T(1,128)} %lengths.1, bf16[256,1536]{1,0:T(8,128)(2,1)} %x_ref.1, ...), custom_call_target="tpu_custom_call" | custom-call | tf_op jit(solution)/shard_map/residual_block/pallas_call | solution.py:890
  184.9 5.6 %finish.1 = (f32[256,1536]{1,0:T(8,128)}, f32[256,1536]{1,0:T(8,128)}, f32[1536]{0:T(1024)}, f32[48,768]{1,0:T(8,128)}, f32[48,768]{1,0:T(8,128)}, /*index=5*/f3...) custom-call(f32[256,1536]{1,0:T(8,128)} %get-tuple-element.40.branch, ...), custom_call_target="tpu_custom_call" | custom-call | tf_op jit(solution)/shard_map/finish/pallas_call | solution.py:911

commit v2 on v1

--- a/solution.py
+++ b/solution.py
@@ -28,6 +28,15 @@
     return sg,[None]+[(seg_of(ri-j,ends)==sg) for j in (1,2,3)]
 def pair_cols(a,j,lo):
     return jnp.where(lo,a[:,2*j:2*j+1],a[:,2*j+1:2*j+2])
+def split(v):
+    high=v.astype(bf16)
+    return high,(v-high.astype(f32)).astype(bf16)
+def row_sums(tri,v,lane):
+    a,rest=split(v)
+    b=(v-a.astype(f32)-rest.astype(f32))
+    packed=a.astype(f32)+pltpu.roll(rest.astype(f32),16,1)+pltpu.roll(b.astype(bf16).astype(f32),32,1)
+    r=nn(tri.astype(bf16),packed.astype(bf16))
+    return r+pltpu.roll(r,112,1)+pltpu.roll(r,96,1)
 def taps(w,masks,halo):
     out=[w[halo:halo+L]]
     for q in (1,2,3):
@@ -44,7 +53,7 @@
     return dtp,dt
 def chunk_decay(ends,r0,dt,hv,ltri):
     dA=dt*hv[1:2,:]
-    cs=nn(ltri,dA,HI)
+    cs=row_sums(ltri,dA,None)
     return dA,cs
 def seg_scalars(ends,r0):
     before=seg_of(r0-1,ends); last=seg_of(r0+L-1,ends)
@@ -56,13 +65,13 @@
     kd=jnp.exp(csl)*jnp.where(before==last,1.0,0.0)
     return e,w,kd
 
-def fwd_chunk(c,ends,nx,wa,pv,pb,hv,ix16,ixh,tmp,ibc,sraw,pre,mixed,yi,sin,bc16,S):
+def fwd_chunk(c,ends,nx,wa,pv,pb,hv,ix16,ixh,tmp,ibc,sraw,pre,mixed,yi,sin,bc16,csum,S):
     r0=pl.multiple_of(c*L,L); rp=pl.multiple_of(c*L+HALO,8)
     rows=pl.ds(r0,L); rows_p=pl.ds(rp,L)
     n=nx[c]
     t=nn(n,wa[:,:,:,0:W].reshape(D,W))
     tmp[...]=t
-    ix16[pl.ds(pl.multiple_of(c*L+16,16),L),:]=t.astype(bf16)
+    ix16[rows,:]=t.astype(bf16)
     t=nn(n,wa[:,:,:,W:].reshape(D,384))
     ibc[rows_p,:]=t[:,:256]
     sraw[rows,:]=t[:,256:]
@@ -73,6 +82,7 @@
     ltri=(ti>=si).astype(f32)
     dtp,dt=head_steps(sraw[rows,:],hv)
     dA,cs=chunk_decay(ends,r0,dt,hv,ltri)
+    csum[rows,:]=cs
     csT=cs.T
     before,last=seg_scalars(ends,r0)
     e,w,kd=chunk_state_decays(cs,sg,before,last)
@@ -112,8 +122,8 @@
         uw=(u*pair_cols(w,j,lo)).astype(bf16)
         S[:,cols]=pair_cols(kd,j,lo[:1])*Sj+nn(BT,uw)
 
-def bwd_chunk(c,ends,pv,pb,hv,ix16,ibc,sraw,pre,mixed,yi,sin,bc16,gm,dS,
-              q1,q3,dpre,rx,dbc,rstep,dk,hs):
+def bwd_chunk(c,ends,pv,pb,hv,ix16,ibc,sraw,pre,mixed,yi,sin,bc16,csum,gm,dS,
+              qs,he,dpre,rx,dbc,rstep,dk,hs):
     r0=pl.multiple_of(c*L,L)
     rows=pl.ds(r0,L)
     lane=iota((L,128),1); lo=lane<64
@@ -122,9 +132,9 @@
     up=[None]+[((seg_of(ri+j,ends)==sg)&(ri+j<T)) for j in (1,2,3)]
     ti=iota((L,L),0); si=iota((L,L),1)
     maskT=(seg_of(ti+r0,ends)==seg_of(si+r0,ends))&(si>=ti)
-    ltri=(ti>=si).astype(f32)
     dtp,dt=head_steps(sraw[rows,:],hv)
-    dA,cs=chunk_decay(ends,r0,dt,hv,ltri)
+    dA=dt*hv[1:2,:]
+    cs=csum[rows,:]
     csT=cs.T
     before,last=seg_scalars(ends,r0)
     e,w,kd=chunk_state_decays(cs,sg,before,last)
@@ -132,7 +142,6 @@
     CT=C.T
     scT=nt(B,C)
     acc=jnp.zeros((L,L),f32); dCin=jnp.zeros((L,N),f32); dBout=jnp.zeros((L,N),f32)
-    win=pl.ds(r0,L+16)
     rowq=[]
     for j in range(NP):
         cols=slice(128*j,128*j+128)
@@ -161,36 +170,39 @@
         yij=yi[rows,cols]
         y_in=mixed[rows,cols]-yij-sk*xc
         udo=u*duo
-        q1[:,cols]=(gb.astype(f32)*yij-ub.astype(f32)*du)+(g*y_in-udo)
+        qs[0,:,cols],qs[1,:,cols]=split((gb.astype(f32)*yij-ub.astype(f32)*du)+(g*y_in-udo))
         du=du+duo
-        q3[:,cols]=xc*du
+        qs[2,:,cols],qs[3,:,cols]=split(xc*du)
         kdj=pair_cols(kd,j,lo[:1])
         rowq.append(jnp.sum(udo,0,keepdims=True)+jnp.sum(kdj*Sb.astype(f32)*dSj,0,keepdims=True))
         dS[:,cols]=kdj*dSj+nn(CT,ge)
         dxc=dtx*du+sk*g
         dp=dxc*(s*(1.0+p*(1.0-s)))
-        ws=taps(ix16[win,cols].astype(f32),masks,16)
+        v=ix16[rows,cols].astype(f32)
         dk[4:5,cols]+=jnp.sum(dp,0,keepdims=True)
         dk[5:6,cols]+=jnp.sum(g*xc,0,keepdims=True)
-        for t_ in range(4):
-            dk[3-t_:4-t_,cols]+=jnp.sum(dp*ws[t_],0,keepdims=True)
+        dk[3:4,cols]+=jnp.sum(dp*v,0,keepdims=True)
         wd=jnp.concatenate([dp,dpre[:,cols]],axis=0)
         dpre[:,cols]=dp[0:HALO]
         dv=pv[3:4,cols]*dp
         for t_ in (1,2,3):
-            dv=dv+pv[3-t_:4-t_,cols]*jnp.where(up[t_],wd[t_:t_+L],0.0)
+            later=jnp.where(up[t_],wd[t_:t_+L],0.0)
+            dk[3-t_:4-t_,cols]+=jnp.sum(later*v,0,keepdims=True)
+            dv=dv+pv[3-t_:4-t_,cols]*later
         rx[c,:,cols]=dv.astype(bf16)
     ab=acc.astype(bf16)
     dbc[:,0:128]=nn(ab,C)+dBout
     dbc[:,128:256]=nn(ab.T,B)+dCin
-    he=((iota((W,128),0)//64)==iota((W,128),1)).astype(f32)
-    dcs=nn(q1[...],he,HI)
-    tailv=nn(jnp.broadcast_to(jnp.concatenate(rowq,axis=1),(8,W)),he,HI)[0:1,:]
-    dcs=dcs+jnp.where(iota((L,128),0)==L-1,tailv,0.0)
-    ddA=nn((si>=ti).astype(f32),dcs,HI)
-    ddt=nn(q3[...],he,HI)+hv[1:2,:]*ddA
+    own=lane<12
+    r=nn(qs[0],he[0])+nn(qs[1],he[0])+nn(qs[2],he[1])+nn(qs[3],he[1])
+    high,low=split(jnp.concatenate(rowq,axis=1))
+    tails=jnp.concatenate([high.astype(f32),low.astype(f32),jnp.zeros((14,W),f32)],axis=0).astype(bf16)
+    tails=nn(tails,he[0])
+    dcs=r+jnp.where(iota((L,128),0)==L-1,tails[0:1,:]+tails[1:2,:],0.0)
+    ddA=row_sums(si>=ti,jnp.where(own,dcs,0.0),None)
+    ddt=pltpu.roll(r,96,1)+hv[1:2,:]*ddA
     hs[1:2,:]+=jnp.sum(ddA*dA,0,keepdims=True)
-    dsr=ddt*sig(dtp)
+    dsr=jnp.where(own,ddt*sig(dtp),0.0)
     hs[0:1,:]+=jnp.sum(dsr,0,keepdims=True)
     rstep[c]=dsr.astype(bf16)
 MESH = pl.DeviceIdType.MESH
@@ -406,7 +418,7 @@
         self.copies[k].start()
 
     def send_far(self):
-        self.copies[0].wait()
+        self.copies[0].wait_recv()
 
         @pl.loop(0, 4)
         def _(k):
@@ -417,6 +429,7 @@
         self.out.start()
 
     def finish(self):
+        self.copies[0].wait_send()
         self.copies[1].wait()
         self.out.wait()
 
@@ -451,9 +464,9 @@
 def mega_kernel(lengths, xloc, cotloc, w_z, w_x, w_bc, w_dt, w_out, norm_gain, conv_x, conv_x_bias, conv_bc, conv_bc_bias,
                 dt_bias, a_log, skip_d, gate_norm,
                 branch_out, gn_out, wz_grad, wx_grad, wo_grad, wbc_grad, wdt_grad, small_out,
-                gain, pv, pb, hv, xg, nx, cot, wa, wz, wo, ix16, ixh, q1, q3, ibc, sraw, pre, mixed, yi, gate, gno, rgate, no, sin, bc16, rstep, S,
+                gain, pv, pb, hv, xg, nx, cot, wa, wz, wo, ix16, ixh, qs, he, csum, ibc, sraw, pre, mixed, yi, gate, gno, rgate, no, sin, bc16, rstep, S,
                 dpre, dk, hs, dbc, ssx, crx, near, far, stz, got1, got2, got3,
-                stb, bot3, dsend, drecv, rbc, bhalo, small, sx, sy, sz, stt, wbx,
+                stb, bot3, dsend, drecv, rmix, bhalo, small, ax, ay, az, bt, bz, bx, by, wbx,
                 asem, bsem, tsem, xsem, csem, osem, gsem, esem, dsem, zsem, wsem, vsem, usem, msem, hsem):
     p = Peers()
     zh, c, me = p.zh, p.c, p.rank
@@ -489,7 +502,10 @@
     hv[0:1, 0:12] = dt_bias[...].reshape(1, 12)
     hv[1:2, 0:12] = -jnp.exp(a_log[...].reshape(1, 12))
     ixh[...] = jnp.zeros((HALO, W), f32)
-    ix16[0:16, :] = jnp.zeros((16, W), bf16)
+    lane = iota((W, 128), 1)
+    head = iota((W, 128), 0) // 64
+    he[0] = jnp.where(lane == head, 1.0, 0.0).astype(bf16)
+    he[1] = jnp.where(lane == head + 32, 1.0, 0.0).astype(bf16)
     ibc[0:HALO, :] = jnp.zeros((HALO, 256), f32)
     S[...] = jnp.zeros((N, W), f32)
     dk[...] = jnp.zeros((16, W), f32)
@@ -524,7 +540,7 @@
 
     @pl.loop(0, NC)
     def _(i):
-        fwd_chunk(i, ends, nx, wa, pv, pb, hv, ix16, ixh, q1, ibc, sraw, pre, mixed, yi, sin, bc16, S)
+        fwd_chunk(i, ends, nx, wa, pv, pb, hv, ix16, ixh, gate.at[pl.ds(0, L), :], ibc, sraw, pre, mixed, yi, sin, bc16, csum, S)
 
         @pl.when(i == 0)
         def _():
@@ -595,8 +611,8 @@
             dk[6:7, cols] += jnp.sum(go * scaled, 0, keepdims=True)
             cross = cross + go * gn * gated
         crx[me, :, rows] = jnp.broadcast_to(row_of(cross), (8, L))
-        for k in range(4):
-            xg[t, :, 384 * k:384 * k + 384] = nt(no[t], wo[k].reshape(384, W)).astype(bf16)
+        for k in range(2):
+            xg[t, :, W * k:W * k + W] = nt(no[t], wo[2 * k:2 * k + 2].reshape(W, W)).astype(bf16)
 
         @pl.when(i == 0)
         def _():
@@ -607,6 +623,7 @@
             out.send_near(1)
 
     e_cross.start()
+    out.send_far()
 
     def weight_part(rows_ref, grads, store):
         @pl.loop(0, 4)
@@ -621,7 +638,6 @@
     weight_part(cot, no, store_wo)
     so = WeightScatter(wo, got1.at[0], got2.at[0], got3.at[0], 384, wsem, p)
     so.first()
-    out.send_far()
     e_cross.wait()
 
     @pl.loop(0, NC)
@@ -650,166 +666,194 @@
 
     S[...] = jnp.zeros((N, W), f32)
     dpre[...] = jnp.zeros((HALO, W), f32)
-    dsend[...] = jnp.zeros((4, 512, 128), bf16)
 
     branch_copies = [
         pltpu.make_async_copy(gate.at[pl.ds(L * h, L), :], branch_out.at[:, pl.ds(W * h, W)], hsem.at[h]) for h in range(2)
     ]
 
-    @pl.loop(0, NC)
-    def _(i):
-        bwd_chunk(NC - 1 - i, ends, pv, pb, hv, ix16, ibc, sraw, pre, mixed, yi, sin, bc16, gno,
-                  S, q1, q3, dpre, no, dbc, rstep, dk, hs)
-        upper = (NC - 1 - i) // 2
-        part = pl.ds(pl.multiple_of(lax.rem(NC - 1 - i, 2) * L, L), L)
-        half = iota((L, 128), 1) // 64
-        for z in range(2):
-            v = dbc[:, 128 * z:128 * z + 128]
-            turned = pltpu.roll(v, 64, 1)
-            for k in range(2):
-                new = jnp.where(upper == k, v, turned)
-                old = dsend[2 * z + k, part, :].astype(f32)
-                dsend[2 * z + k, part, :] = jnp.where(half == upper, new, old).astype(bf16)
-
-        @pl.when(i == 0)
-        def _():
-            so.second()
-            out.finish()
-            live = iota((L, 128), 0) + me * L < ends[3]
-            for j in range(2 * NP):
-                cols = slice(128 * j, 128 * j + 128)
-                gate[L * (j // NP):L * (j // NP) + L, 128 * (j % NP):128 * (j % NP) + 128] = jnp.where(
-                    live, out.total(slice(None), cols), 0.0)
-            start_all(branch_copies)
-
-        @pl.when(i == 1)
-        def _():
-            so.third()
-            sz_.second()
-
-        @pl.when(i == 2)
-        def _():
-            sz_.third()
-
     ranks = [zh * 2 + 1 - c, (1 - zh) * 2 + c, (1 - zh) * 2 + 1 - c]
-    dcopies = [remote(dsend.at[r], drecv.at[k], dsem, k, to) for k, (r, to) in enumerate(zip(ranks, p.group))]
-    start_all(dcopies)
-
-    wo_grad[...] = so.finish()
-    wz_grad[...] = sz_.finish()
-    weight_part(nx, no, store_z)
-    sx_ = WeightScatter(stz, got1.at[1], got2.at[1], got3.at[2], 384, vsem, p)
-    sx_.first()
-    wait_all(dcopies)
-
-    bhalo[...] = jnp.zeros((HALO, 128), f32)
     tile = pl.ds(pl.multiple_of(zh * 128, 128), 128)
     half = (iota((L, 128), 1) // 64) == c
-
-    @pl.loop(0, NC)
-    def _(k):
-        i = NC - 1 - k
-        r0 = pl.multiple_of(i * L, L)
-        part = pl.ds(pl.multiple_of(lax.rem(i, 2) * L, L), L)
+    bhalo[...] = jnp.zeros((HALO, 128), f32)
+    for k in range(4):
+        bc_tile = wa[k, :, :, pl.ds(pl.multiple_of(W + zh * 128, 128), 128)].reshape(384, 128).astype(f32)
+        dt_tile = wa[k, :, :, W + 256:].reshape(384, 128).astype(f32)
+        dt_tile = jnp.where(c == 0, pltpu.roll(dt_tile, 64, 1), dt_tile)
+        mix = jnp.where((iota((384, 128), 1) // 64) == c, bc_tile, dt_tile)
+        stb[k] = mix.astype(bf16).reshape(4, 96, 128)
+    gn_sum = RowScatter(cot, near, far, gsem, p)
+    across = (1 - zh) * 2 + c
+
+    def bc_copies(q):
+        return [remote(dsend.at[q, r], drecv.at[q, k], dsem, 3 * q + k, to) for k, (r, to) in enumerate(zip(ranks, p.group))]
+
+    def pack(q):
+        low = iota((128, 128), 1) < 64
+        for z in range(2):
+            cols = slice(128 * z, 128 * z + 128)
+            top, bottom = dbc[0:128, cols], dbc[128:256, cols]
+            dsend[q, 2 * z] = jnp.where(low, top, pltpu.roll(bottom, 64, 1)).astype(bf16)
+            dsend[q, 2 * z + 1] = jnp.where(low, pltpu.roll(top, 64, 1), bottom).astype(bf16)
+
+    def conv_back(q):
+        r0 = pl.multiple_of(q * L, L)
         sg, masks = chunk_masks(ends, r0)
         ri = iota((L, 128), 0) + r0
-        packed = dsend[me, part, :].astype(f32)
-        for q in range(3):
-            packed = packed + drecv[q, part, :].astype(f32)
-        moved = jnp.where(i // 2 == c, packed, pltpu.roll(packed, 64, 1))
-        grad = jnp.where(half, moved, 0.0)
+        packed = dsend[q, me].astype(f32)
+        for k in range(3):
+            packed = packed + drecv[q, k].astype(f32)
+        turned = pltpu.roll(packed, 64, 1)
+        both = jnp.concatenate([jnp.where(c == 0, packed, turned), jnp.where(c == 0, turned, packed)], axis=0)
+        grad = jnp.where(half, both, 0.0)
         kernel = pb[:, tile]
         ws = taps(ibc[pl.ds(r0, L + HALO), tile], masks, HALO)
         pre_bc = kernel[4:5] + kernel[3:4] * ws[0] + kernel[2:3] * ws[1] + kernel[1:2] * ws[2] + kernel[0:1] * ws[3]
         s = sig(pre_bc)
         dp = grad * (s * (1.0 + pre_bc * (1.0 - s)))
-        for t in range(4):
-            cols = pl.ds(pl.multiple_of((3 - t) % 3 * 256 + zh * 128, 128), 128)
-            row = 10 if t else 11
-            small[row:row + 1, cols] += jnp.sum(dp * ws[t], 0, keepdims=True)
         cols = pl.ds(pl.multiple_of(256 + zh * 128, 128), 128)
         small[11:12, cols] += jnp.sum(dp, 0, keepdims=True)
         wd = jnp.concatenate([dp, bhalo[...]], axis=0)
         bhalo[...] = dp[0:HALO]
-        dv = kernel[3:4] * dp
-        for t in (1, 2, 3):
-            same = (seg_of(ri + t, ends) == sg) & (ri + t < T)
-            dv = dv + kernel[3 - t:4 - t] * jnp.where(same, wd[t:t + L], 0.0)
-        rbc[0, i] = dv.astype(bf16)
-        step = rstep[i].astype(f32)
-        rbc[1, i] = (dv + jnp.where(half, 0.0, jnp.where(c == 0, pltpu.roll(step, 64, 1), step))).astype(bf16)
+        dv = jnp.zeros((L, 128), f32)
+        for t in range(4):
+            later = dp
+            if t:
+                later = jnp.where((seg_of(ri + t, ends) == sg) & (ri + t < T), wd[t:t + L], 0.0)
+            dv = dv + kernel[3 - t:4 - t] * later
+            cols = pl.ds(pl.multiple_of((3 - t) % 3 * 256 + zh * 128, 128), 128)
+            row = 10 if t else 11
+            small[row:row + 1, cols] += jnp.sum(later * ws[0], 0, keepdims=True)
+        step = rstep[q].astype(f32)
+        rmix[q] = (dv + jnp.where(half, 0.0, jnp.where(c == 0, pltpu.roll(step, 64, 1), step))).astype(bf16)
+
+    def normed_grad(q):
+        for k in range(2):
+            cols = slice(W * k, W * k + W)
+            total = nt(rgate[q], wz[2 * k:2 * k + 2].reshape(W, W))
+            total = total + nt(no[q], wa[2 * k:2 * k + 2, :, :, 0:W].reshape(W, W))
+            total = total + nt(rmix[q], stb[2 * k:2 * k + 2].reshape(W, 128))
+            cot[q, :, cols] = total.astype(bf16)
+            weighted = jnp.sum(total * nx[q, :, cols].astype(f32), 0, keepdims=True) / gain[0:1, cols]
+            small[8 + k:9 + k, :] += weighted
+
+        @pl.when(q == (1 - zh) * 2 + 1 - c)
+        def _():
+            gn_sum.send_near(0)
+
+        @pl.when(q == zh * 2 + 1 - c)
+        def _():
+            gn_sum.send_near(1)
+
+    branch_copies = [
+        pltpu.make_async_copy(gate.at[pl.ds(L * h, L), :], branch_out.at[:, pl.ds(W * h, W)], hsem.at[h]) for h in range(2)
+    ]
+    a_x = Exchange(ax, p.x, p.along_x, msem, 0)
+    a_y = Exchange(ay, p.y, p.along_y, msem, 3)
+    a_z = Exchange(az, p.zl, [p.pair], msem, 6)
+    b_t = Exchange(bt, me, p.group, msem, 7)
+    b_z = Exchange(bz, p.zl, [p.pair], msem, 10)
+    b_x = Exchange(bx, p.x, p.along_x, msem, 11)
+    b_y = Exchange(by, p.y, p.along_y, msem, 14)
+    sx_ = WeightScatter(wo, got1.at[0], got2.at[0], got3.at[2], 384, vsem, p)
+
+    @pl.loop(0, NC + 1)
+    def _(i):
+        @pl.when(i < NC)
+        def _():
+            q = NC - 1 - i
+            bwd_chunk(q, ends, pv, pb, hv, ix16, ibc, sraw, pre, mixed, yi, sin, bc16, csum, gno,
+                      S, qs, he, dpre, no, dbc, rstep, dk, hs)
+            pack(q)
+
+            @pl.when(i == 0)
+            def _():
+                out.finish()
+                live = iota((L, 128), 0) + me * L < ends[3]
+                for j in range(2 * NP):
+                    cols = slice(128 * j, 128 * j + 128)
+                    gate[L * (j // NP):L * (j // NP) + L, 128 * (j % NP):128 * (j % NP) + 128] = jnp.where(
+                        live, out.total(slice(None), cols), 0.0)
+                start_all(branch_copies)
+
+            start_all(bc_copies(q))
+
+            @pl.when(i == 1)
+            def _():
+                so.second()
+
+            @pl.when(i == 2)
+            def _():
+                so.third()
+                sz_.second()
+
+            @pl.when(i == 3)
+            def _():
+                sz_.third()
+
+        @pl.when(i == NC)
+        def _():
+            small[0:7, :] = dk[0:7, :]
+            small[7:8, 0:128] = hs[0:1, :]
+            small[7:8, 128:256] = hs[1:2, :]
+            ax[p.x] = small[0:8, :]
+            a_x.start()
+            wo_grad[...] = so.finish()
+            weight_part(nx, no, store_wo)
+            a_x.wait()
+            ay[p.y] = ax[0] + ax[1] + ax[2] + ax[3]
+            a_y.start()
+            sx_.first()
+
+        @pl.when((i > 1) & (NC + 1 - i == across))
+        def _():
+            gn_sum.send_far()
+
+        @pl.when(i > 0)
+        def _():
+            wait_all(bc_copies(NC - i))
+            conv_back(NC - i)
+            normed_grad(NC - i)
+
+    bt[me] = small[8:16, :]
+    b_t.start()
 
     def store_b(b, v):
         stb[b] = v
 
-    weight_part(nx, rbc.at[1], store_b)
+    weight_part(nx, rmix, store_b)
     low_cols = pl.ds(0, 128)
-    sb_ = WeightScatter(stb, got1.at[0, :, :, :, low_cols], got2.at[0, :, :, low_cols], bot3, 128, usem, p)
+    sb_ = WeightScatter(stb, got1.at[1, :, :, :, low_cols], got2.at[1, :, :, low_cols], bot3, 128, usem, p)
     sb_.first()
 
-    gn_sum = RowScatter(cot, near, far, gsem, p)
-    small[8:10, :] = jnp.zeros((2, W), f32)
-
-    @pl.loop(0, NC)
-    def _(i):
-        t = jnp.where(i < 2, 1 - zh, zh) * 2 + jnp.where(lax.rem(i, 2) == 0, 1 - c, c)
-        for k in range(4):
-            cols = slice(384 * k, 384 * k + 384)
-            total = nt(rgate[t], wz[k].reshape(384, W))
-            total = total + nt(no[t], wa[k, :, :, 0:W].reshape(384, W))
-            total = total + nt(rstep[t], wa[k, :, :, W + 256:].reshape(384, 128))
-            total = total + nt(rbc[0, t], wa[k, :, :, pl.ds(pl.multiple_of(W + zh * 128, 128), 128)].reshape(384, 128))
-            cot[t, :, cols] = total.astype(bf16)
-            weighted = jnp.sum(total * nx[t, :, cols].astype(f32), 0, keepdims=True) / gain[0:1, cols]
-            small[8 + k // 2:9 + k // 2, 384 * (k % 2):384 * (k % 2) + 384] += weighted
-
-        @pl.when(i == 0)
-        def _():
-            gn_sum.send_near(0)
-
-        @pl.when(i == 1)
-        def _():
-            gn_sum.send_far()
-
-        @pl.when(i == 2)
-        def _():
-            gn_sum.send_near(1)
-
-    small[0:7, :] = dk[0:7, :]
-    small[7:8, 0:128] = hs[0:1, :]
-    small[7:8, 128:256] = hs[1:2, :]
-    sx[p.x] = small[...]
-    e_x = Exchange(sx, p.x, p.along_x, msem, 0)
-    e_x.start()
+    @pl.when(across == 0)
+    def _():
+        gn_sum.send_far()
+
+    a_y.wait()
+    az[p.zl] = ay[0] + ay[1] + ay[2] + ay[3]
+    a_z.start()
+    b_t.wait()
+    bz[p.zl] = bt[0] + bt[1] + bt[2] + bt[3]
+    b_z.start()
+    wz_grad[...] = sz_.finish()
+    a_z.wait()
+    small_out[0:8, :] = az[0] + az[1]
+    b_z.wait()
+    bx[p.x] = bz[0] + bz[1]
+    b_x.start()
+    sb_.second()
     sx_.second()
-    sb_.second()
-    e_x.wait()
-    sy[p.y] = sx[0] + sx[1] + sx[2] + sx[3]
-    e_y = Exchange(sy, p.y, p.along_y, msem, 3)
-    e_y.start()
-    e_y.wait()
-    sz[p.zl] = sy[0] + sy[1] + sy[2] + sy[3]
-    e_z = Exchange(sz, p.zl, [p.pair], msem, 6)
-    e_z.start()
+    b_x.wait()
+    by[p.y] = bx[0] + bx[1] + bx[2] + bx[3]
+    b_y.start()
     sb_.third()
     sx_.third()
-    e_z.wait()
-    small_out[...] = sz[0] + sz[1]
-    stt[me] = small_out[8:16, :]
-    e_t = Exchange(stt, me, p.group, msem, 7)
-    e_t.start()
+    b_y.wait()
+    small_out[8:16, :] = by[0] + by[1] + by[2] + by[3]
     wbx[me] = sb_.finish()
-    e_b = Exchange(wbx, me, p.group, msem, 10)
+    e_b = Exchange(wbx, me, p.group, msem, 17)
     e_b.start()
     wx_grad[...] = sx_.finish()
-    e_t.wait()
-    small_out[8:16, :] = stt[0] + stt[1] + stt[2] + stt[3]
-    e_b.wait()
-    low = iota((48, 128), 1) < 64
-    wbc_grad[:, 0:128] = jnp.where(low, wbx[0], wbx[1])
-    wbc_grad[:, 128:256] = jnp.where(low, wbx[2], wbx[3])
-    mine = wbx[me]
-    wdt_grad[...] = jnp.where(c == 0, pltpu.roll(mine, 64, 1), mine)
     gn_sum.finish()
     for j in range(2 * NP):
         cols = slice(128 * j, 128 * j + 128)
@@ -819,6 +863,12 @@
         for h in range(2)
     ]
     start_all(gn_copies)
+    e_b.wait()
+    low = iota((48, 128), 1) < 64
+    wbc_grad[:, 0:128] = jnp.where(low, wbx[0], wbx[1])
+    wbc_grad[:, 128:256] = jnp.where(low, wbx[2], wbx[3])
+    mine = wbx[me]
+    wdt_grad[...] = jnp.where(c == 0, pltpu.roll(mine, 64, 1), mine)
     wait_all(branch_copies)
     wait_all(gn_copies)
 
@@ -871,7 +921,7 @@
     rows4 = V((4, 256, D), bf16)
     scratch = dict(
         gain=V((8, D), f32), pv=V((16, W), f32), pb=V((8, 256), f32), hv=V((8, 128), f32), xg=rows4, nx=rows4, cot=rows4, wa=V((4, 4, 96, 1152), bf16), wz=V((4, 4, 96, W), bf16), wo=V((4, 4, 96, W), bf16),
-        ix16=V((T + 16, W), bf16), ixh=V((HALO, W), f32), q1=V((L, W), f32), q3=V((L, W), f32),
+        ix16=V((T, W), bf16), ixh=V((HALO, W), f32), qs=V((4, L, W), bf16), he=V((2, W, 128), bf16), csum=V((T, 128), f32),
         ibc=V((T + HALO, 256), f32), sraw=V((T, 128), f32), pre=V((T, W), f32), mixed=V((T, W), f32), yi=V((T, W), f32),
         gate=V((T, W), f32), gno=V((T, W), f32), rgate=V((4, L, W), bf16), no=V((4, L, W), bf16),
         sin=V((NC, N, W), bf16), bc16=V((T, 256), bf16), rstep=V((4, L, 128), bf16), S=V((N, W), f32),
@@ -880,11 +930,12 @@
         near=V((2, L, D), bf16), far=V((L, D), bf16),
         stz=V((4, 4, 96, W), bf16), got1=V((2, 3, 4, 96, W), bf16), got2=V((2, 3, 96, W), bf16), got3=V((3, 48, W), bf16),
         stb=V((4, 4, 96, 128), bf16), bot3=V((48, 128), bf16),
-        dsend=V((4, 512, 128), bf16), drecv=V((3, 512, 128), bf16), rbc=V((2, 4, L, 128), bf16), bhalo=V((HALO, 128), f32),
-        small=V((16, W), f32), sx=V((4, 16, W), f32), sy=V((4, 16, W), f32), sz=V((2, 16, W), f32), stt=V((4, 8, W), f32),
+        dsend=V((4, 4, 128, 128), bf16), drecv=V((4, 3, 128, 128), bf16), rmix=V((4, L, 128), bf16), bhalo=V((HALO, 128), f32),
+        small=V((16, W), f32), ax=V((4, 8, W), f32), ay=V((4, 8, W), f32), az=V((2, 8, W), f32), bt=V((4, 8, W), f32), bz=V((2, 8, W), f32),
+        bx=V((4, 8, W), f32), by=V((4, 8, W), f32),
         wbx=V((4, 48, 128), f32),
-        asem=sems(21), bsem=sems(21), tsem=sems(21), xsem=sems(4), csem=sems(4), osem=sems(3), gsem=sems(3), esem=sems(6), dsem=sems(3),
-        zsem=sems(13), wsem=sems(13), vsem=sems(13), usem=sems(13), msem=sems(13),
+        asem=sems(21), bsem=sems(21), tsem=sems(21), xsem=sems(4), csem=sems(4), osem=sems(3), gsem=sems(3), esem=sems(6), dsem=sems(12),
+        zsem=sems(13), wsem=sems(13), vsem=sems(13), usem=sems(13), msem=sems(20),
         hsem=pltpu.SemaphoreType.DMA((4,)),
     )
     return pl.pallas_call(

time: 191 us -> 177 us (0.927)
  Pallas kernels: 190 us -> 176 us
    pallas_call x1, Pallas kernels: 184 us -> 170 us  [block(): pl.pallas_call(mega_kernel, out_shape=[shape((256, D), f32), shape((256,...]
where the time goes in v2:
time: 177 us
  Pallas kernels  176 us (99%)
    pallas_call x1, Pallas kernels, block(): pl.pallas_call(mega_kernel, out_shape=[shape((256, D), f32), shape((256,...  170 us
    pallas_call x1, Pallas kernels, finish(): pl.pallas_call(finish_kernel, grid=(4,), out_shape=[shape((256, D), f32)]...  5.64 us

profile of v2, /device:TPU:1, one launch (start us, length us, event | category | flops | bytes accessed | tf_op | source)
XLA Modules:
  0.0 176.5 jit_solution(4872103852638736499)
XLA Ops:
  0.7 170.1 %residual_block.1 = (f32[256,1536]{1,0:T(8,128)}, f32[256,1536]{1,0:T(8,128)}, f32[48,768]{1,0:T(8,128)}, f32[48,768]{1,0:T(8,128)}, f32[48,768]{1,0:T(8,128)}, ...) custom-call(s32[1,4]{1,0:T(1,128)} %lengths.1, bf16[256,1536]{1,0:T(8,128)(2,1)} %x_ref.1, ...), custom_call_target="tpu_custom_call" | custom-call | tf_op jit(solution)/shard_map/residual_block/pallas_call | solution.py:941
  170.7 5.6 %finish.1 = (f32[256,1536]{1,0:T(8,128)}, f32[256,1536]{1,0:T(8,128)}, f32[1536]{0:T(1024)}, f32[48,768]{1,0:T(8,128)}, f32[48,768]{1,0:T(8,128)}, /*index=5*/f3...) custom-call(f32[256,1536]{1,0:T(8,128)} %get-tuple-element.40.branch, ...), custom_call_target="tpu_custom_call" | custom-call | tf_op jit(solution)/shard_map/finish/pallas_call | solution.py:962

commit v3 on v2

--- a/solution.py
+++ b/solution.py
@@ -837,7 +837,12 @@
     b_z.start()
     wz_grad[...] = sz_.finish()
     a_z.wait()
-    small_out[0:8, :] = az[0] + az[1]
+    total = az[0] + az[1]
+    small_out[0:8, :] = total
+    high, low = split(total[5:6, :])
+    pair = jnp.concatenate([high.astype(f32), low.astype(f32), jnp.zeros((14, W), f32)], axis=0).astype(bf16)
+    pair = nn(pair, he[0])
+    small_out[7:8, 256:384] = pair[0:1, :] + pair[1:2, :]
     b_z.wait()
     bx[p.x] = bz[0] + bz[1]
     b_x.start()
@@ -892,9 +897,7 @@
         wdt_grad[...] = jnp.concatenate([wdt[...], jnp.zeros((80, 128), f32)], axis=0).T[0:12, 0:48]
         conv_x[...] = small[0:4, :]
         conv_x_bias[...] = small[4:5, :].reshape(W)
-        he = ((iota((W, 128), 0) // 64) == iota((W, 128), 1)).astype(f32)
-        sums = nn(jnp.broadcast_to(small[5:6, :], (8, W)), he, HI)
-        skip[...] = sums[0:1, 0:12].reshape(12)
+        skip[...] = small[7:8, 256:268].reshape(12)
         gate_norm[...] = small[6:7, :].reshape(W)
         dt_bias[...] = small[7:8, 0:12].reshape(12)
         a_log[...] = small[7:8, 128:140].reshape(12)
@@ -953,7 +956,7 @@
 
 
 def finish(*args):
-    rows = pl.BlockSpec((64, D), lambda i: (i, 0))
+    rows = pl.BlockSpec((128, D), lambda i: (i, 0))
 
     def whole(*dims):
         return pl.BlockSpec(dims, lambda i: (0,) * len(dims))
@@ -961,7 +964,7 @@
     outs = [(D,), (48, W), (48, W), (48, 256), (12, 48), (4, W), (W,), (4, 256), (256,), (12,), (12,), (12,), (W,), (48, W)]
     return pl.pallas_call(
         finish_kernel,
-        grid=(4,),
+        grid=(2,),
         out_shape=[shape((256, D), f32)] * 2 + [shape(s, f32) for s in outs],
         in_specs=[rows] * 4 + [whole(D)] + [whole(48, W)] * 3 + [whole(48, 256), whole(48, 128), whole(16, W)],
         out_specs=[rows] * 2 + [whole(*s) for s in outs],

time: 177 us -> 175 us (0.989)
  Pallas kernels: 176 us -> 174 us
where the time goes in v3:
time: 175 us
  Pallas kernels  174 us (99%)
    pallas_call x1, Pallas kernels, block(): pl.pallas_call(mega_kernel, out_shape=[shape((256, D), f32), shape((256,...  170 us
    pallas_call x1, Pallas kernels, finish(): pl.pallas_call(finish_kernel, grid=(2,), out_shape=[shape((256, D), f32)]...  4.3 us

profile of v3, /device:TPU:1, one launch (start us, length us, event | category | flops | bytes accessed | tf_op | source)
XLA Modules:
  0.0 175.2 jit_solution(1457327541868882489)
XLA Ops:
  0.7 170.1 %residual_block.1 = (f32[256,1536]{1,0:T(8,128)}, f32[256,1536]{1,0:T(8,128)}, f32[48,768]{1,0:T(8,128)}, f32[48,768]{1,0:T(8,128)}, f32[48,768]{1,0:T(8,128)}, ...) custom-call(s32[1,4]{1,0:T(1,128)} %lengths.1, bf16[256,1536]{1,0:T(8,128)(2,1)} %x_ref.1, ...), custom_call_target="tpu_custom_call" | custom-call | tf_op jit(solution)/shard_map/residual_block/pallas_call | solution.py:944
  170.7 4.3 %finish.1 = (f32[256,1536]{1,0:T(8,128)}, f32[256,1536]{1,0:T(8,128)}, f32[1536]{0:T(1024)}, f32[48,768]{1,0:T(8,128)}, f32[48,768]{1,0:T(8,128)}, /*index=5*/f3...) custom-call(f32[256,1536]{1,0:T(8,128)} %get-tuple-element.40.branch, ...), custom_call_target="tpu_custom_call" | custom-call | tf_op jit(solution)/shard_map/finish/pallas_call | solution.py:965

commit v4 on v3

--- a/solution.py
+++ b/solution.py
@@ -846,8 +846,8 @@
     b_z.wait()
     bx[p.x] = bz[0] + bz[1]
     b_x.start()
+    sx_.second()
     sb_.second()
-    sx_.second()
     b_x.wait()
     by[p.y] = bx[0] + bx[1] + bx[2] + bx[3]
     b_y.start()

time: 175 us -> 176 us (level)
  no operation moved by 1% of the time
where the time goes in v4:
time: 176 us
  Pallas kernels  175 us (99%)
    pallas_call x1, Pallas kernels, block(): pl.pallas_call(mega_kernel, out_shape=[shape((256, D), f32), shape((256,...  171 us
    pallas_call x1, Pallas kernels, finish(): pl.pallas_call(finish_kernel, grid=(2,), out_shape=[shape((256, D), f32)]...  4.3 us

profile of v4, /device:TPU:1, one launch (start us, length us, event | category | flops | bytes accessed | tf_op | source)
XLA Modules:
  0.0 175.7 jit_solution(11366135844209746385)
XLA Ops:
  0.7 170.6 %residual_block.1 = (f32[256,1536]{1,0:T(8,128)}, f32[256,1536]{1,0:T(8,128)}, f32[48,768]{1,0:T(8,128)}, f32[48,768]{1,0:T(8,128)}, f32[48,768]{1,0:T(8,128)}, ...) custom-call(s32[1,4]{1,0:T(1,128)} %lengths.1, bf16[256,1536]{1,0:T(8,128)(2,1)} %x_ref.1, ...), custom_call_target="tpu_custom_call" | custom-call | tf_op jit(solution)/shard_map/residual_block/pallas_call | solution.py:944
  171.3 4.3 %finish.1 = (f32[256,1536]{1,0:T(8,128)}, f32[256,1536]{1,0:T(8,128)}, f32[1536]{0:T(1024)}, f32[48,768]{1,0:T(8,128)}, f32[48,768]{1,0:T(8,128)}, /*index=5*/f3...) custom-call(f32[256,1536]{1,0:T(8,128)} %get-tuple-element.40.branch, ...), custom_call_target="tpu_custom_call" | custom-call | tf_op jit(solution)/shard_map/finish/pallas_call | solution.py:965
